TPU v7x, 512 devices: a whole 4x4x16 slice. The times are simulated.
512 devices in a mesh: seq: 128 (over y, z, core), head: 4 (over x).
Axes of the slice: x: 4, y: 4, z: 16, core: 2. Of those that a mesh axis runs over, the one named last changes fastest.
Arguments:
- queries: bfloat16 [4, 4, 128, 32], P(None, 'head'), may hold values from -16 to 16
- keys: bfloat16 [4, 4, 128, 131072], P(None, 'head', None, 'seq'), may hold values from -48 to 48
- values: bfloat16 [4, 4, 128, 131072], P(None, 'head', None, 'seq'), may hold values from -6 to 6
- lengths: int32 [4], replicated, may hold values from 65536 to 131072, as said below
- offsets: int32 [4, 4], replicated, may hold values from 0 to 3, as said below
- out_proj: bfloat16 [4, 8, 128, 8192], P('head', None, None, 'seq'), may hold values from -0.23925781 to 0.23925781
Outputs:
- mixed: float32 [4, 4, 8192], P(None, None, 'seq')
Inputs may be any that keep to these rules, and one draw needn't show every extreme that they name: `lengths`: every sequence holds at least 65536 positions; one sequence holds exactly 131072. `offsets`: each row is a permutation of 0 to 3.
All inputs are finite; a program needn't handle non-finite values.
Results may differ from a plain program's by a relative error of at most 0.0031.
Values sent between devices are 32-bit elements; how exact they have to be, the bound alone decides.
No kernel may reach another device: no remote copies, remote signals or barrier semaphores. Data moves between devices by JAX's collectives and lax.ppermute only.
A program may use at most 64 MiB of HBM per device.

v0:
```python
import jax
import jax.numpy as jnp
from jax import lax
from jax.sharding import PartitionSpec as P

masked_score = -1e30


def shards(queries, keys, values, lengths, offsets, out_proj):
    batch_count = keys.shape[0]
    group_count = keys.shape[1]
    head_size = keys.shape[2]
    ctx_dev = keys.shape[3]
    row_count = queries.shape[3]
    draft_count = offsets.shape[1]
    head_count = row_count // draft_count
    scores = jnp.einsum("bgdr,bgdp->bgrp", queries, keys, preferred_element_type=jnp.float32)
    scores = scores * head_size ** (-0.5)
    positions = lax.axis_index("seq") * ctx_dev + jnp.arange(ctx_dev, dtype=jnp.int32)
    visible = jnp.repeat(lengths[:, None] - offsets, head_count, axis=1)
    seen = (positions[None, None, :] < visible[:, :, None])[:, None]
    scores = jnp.where(seen, scores, masked_score)
    block_max = jnp.max(scores, axis=-1)
    weights = jnp.where(seen, jnp.exp(scores - block_max[..., None]), 0.0)
    block_sum = jnp.sum(weights, axis=-1)
    rounded = weights.astype(jnp.bfloat16)
    block_out = jnp.einsum("bgrp,bgdp->bgrd", rounded, values, preferred_element_type=jnp.float32)
    row_top = lax.pmax(block_max, "seq")
    factor = jnp.exp(block_max - row_top)
    denominator, summed = lax.psum((block_sum * factor, block_out * factor[..., None]), "seq")
    attended = (summed / denominator[..., None]).astype(jnp.bfloat16)
    attended = attended.reshape(batch_count, group_count, draft_count, head_count, head_size)
    partial_out = jnp.einsum(
        "bgjhd,ghdc->bjc", attended, out_proj, preferred_element_type=jnp.float32
    )
    return lax.psum(partial_out, "head")


def solution(mesh):
    placed = (
        P(None, "head", None, None),
        P(None, "head", None, "seq"),
        P(None, "head", None, "seq"),
        P(),
        P(),
        P("head", None, None, "seq"),
    )
    return jax.shard_map(
        shards, mesh=mesh, in_specs=placed, out_specs=P(None, None, "seq"), check_vma=False
    )
```

profile of v0, /device:TPU:1, one launch (start us, length us, event | category | flops | bytes accessed | tf_op | source)
XLA Modules:
  0.0 584.2 jit_solution(881070405545237560)
XLA Ops:
  6.5 0.0 copy-start
  6.5 0.0 copy-start.2
  6.5 0.0 all-reduce.2.cloned.1.call-start
  6.5 0.8 broadcast_subtract_fusion
  7.4 0.1 broadcast_in_dim.16
  7.5 0.1 lt.16
  7.5 0.2 copy-done
  7.8 0.0 copy-done.2
  7.8 0.0 copy-start.1
  7.8 0.4 fusion.18
  8.2 254.7 %pmax.7 = f32[4,1,32]{2,0,1:T(4,128)S(1)} all-reduce(f32[4,1,32]{2,0,1:T(4,128)S(1)} %bitcast.35), channel_id=1, replica_groups=mesh['seq'=128,'head'=4] {'seq'}, use_global_device_ids=true, to_apply=%region_1.2 | all-reduce | flops 128 | bytes 1024 | tf_op jit(solution)/shard_map/pmax | solution.py:28
  262.8 0.2 fusion.4
  263.1 0.0 copy-done.1
  263.1 1.1 fusion.1
  264.2 0.0 copy-start.3
  264.2 0.0 all-reduce.2.cloned.1.call-update
  264.3 251.2 %psum.22 = f32[4,32]{1,0:T(4,128)S(1)} all-reduce(f32[4,32]{1,0:T(4,128)S(1)} %get-tuple-element.5), channel_id=1, replica_groups=mesh['seq'=128,'head'=4] {'seq'}, use_global_device_ids=true, to_apply=%region_4.5 | all-reduce | flops 128 | bytes 1024 | tf_op jit(solution)/shard_map/psum | solution.py:30
  515.5 51.6 %all-reduce.2.cloned.1.call-done = f32[4,1,32,128]{3,2,0,1:T(8,128)} async-done(((f32[4,1,32,128]{3,2,0,1:T(8,128)}), f32[4,1,32,128]{3,2,0,1:T(8,128)}) %all-reduce.2.cloned.1.call-update) | async-done | bytes 65552 | tf_op jit(solution)/shard_map/psum | solution.py:30
  567.1 0.9 fusion.14
  568.1 0.0 copy-done.3
  568.1 0.2 convolution_bitcast_fusion
  568.2 9.1 %psum.23 = f32[4,4,64]{2,1,0:T(4,128)} all-reduce(f32[4,4,64]{2,1,0:T(4,128)S(1)} %convolution_bitcast_fusion), channel_id=1, replica_groups=mesh['seq'=128,'head'=4] {'head'}, use_global_device_ids=true, to_apply=%region_5.6 | all-reduce | flops 1024 | bytes 8192 | tf_op jit(solution)/shard_map/psum | solution.py:36
  (2 shorter events, 0.0 us)
Async XLA Ops:
  6.5 1.3 copy-start
  6.5 1.3 copy-start.2
  6.5 560.6 %all-reduce.2.cloned.1.call-start = ((), (), s32[]{:S(2)}) async-start(), calls=%async_computation | async-start | bytes 131072 | tf_op jit(solution)/shard_map/psum | solution.py:30
  7.8 255.3 %copy-start.1 = (bf16[4,1,128,1024]{3,2,1,0:T(8,128)(2,1)S(1)}, bf16[4,1,128,1024]{3,2,1,0:T(8,128)(2,1)}, u32[]{:S(2)}) copy-start(bf16[4,1,128,1024]{3,2,1,0:T(8,128)(2,1)} %param.8) | copy-start | bytes 3145732
  264.2 303.8 %copy-start.3 = (bf16[1,8,128,64]{2,3,1,0:T(8,128)(2,1)S(1)}, bf16[1,8,128,64]{2,3,1,0:T(8,128)(2,1)}, u32[]{:S(2)}) copy-start(bf16[1,8,128,64]{2,3,1,0:T(8,128)(2,1)} %param.11) | copy-start | bytes 393220
Sparse Core Ops, SparseCore 0:
  264.4 302.7 all-reduce.1
where the time goes:
time: 585 us; the launch traced here: 584 us
  blocking collectives  515 us (88%)
  waiting for transfers between devices  51.7 us (9%)
  between operations  13.4 us (2%)
    pmax x1, blocking collectives, shards(): row_top = lax.pmax(block_max, 'seq')  255 us
    psum x1, blocking collectives, shards(): lax.psum((block_sum * factor, block_out * factor[..., None]), 'seq')  251 us
    psum x1, waiting for transfers between devices, shards(): lax.psum((block_sum * factor, block_out * factor[..., None]), 'seq')  51.6 us
  transfers between devices with their start and end apart: 1, of which 1 were waited for; matrix products, arithmetic and copies ran while one was open for 0% of the time, Pallas kernels for 0%

commit v1 on v0

v1 whole, which is shorter than its diff:
```python
import jax
import jax.numpy as jnp
from jax import lax
from jax.experimental import pallas as pl
from jax.experimental.pallas import tpu as pltpu
from jax.sharding import Mesh, PartitionSpec as P

masked_score = -1e30
Y, Z, CORES, HEAD = 4, 16, 2, 4
CHIPS = Y * Z
BATCH, DRAFT, HEADS, ROWS, DH, CTX_DEV, COLS = 4, 4, 8, 32, 128, 1024, 64
HALF = BATCH * ROWS // CORES
LANES = 128
vmem = pl.BlockSpec(memory_space=pltpu.VMEM)
smem = pl.BlockSpec(memory_space=pltpu.SMEM)
hbm = pl.BlockSpec(memory_space=pl.ANY)


def attend_block(lengths, offsets, queries, keys, values, out, held_keys, held_values, key_sems, value_sems):
    def key_copy(b):
        return pltpu.make_async_copy(keys.at[b, 0], held_keys.at[b], key_sems.at[b])

    def value_copy(b):
        return pltpu.make_async_copy(values.at[b, 0], held_values.at[b], value_sems.at[b])

    for b in range(BATCH):
        key_copy(b).start()
        value_copy(b).start()
    index = (lax.axis_index("y") * Z + lax.axis_index("z")) * CORES + lax.axis_index("core")
    positions = index * CTX_DEV + lax.broadcasted_iota(jnp.int32, (ROWS, CTX_DEV), 1)
    draft = lax.broadcasted_iota(jnp.int32, (ROWS, 1), 0) // HEADS
    lane = lax.broadcasted_iota(jnp.int32, (ROWS, LANES), 1)
    for b in range(BATCH):
        key_copy(b).wait()
        scores = lax.dot_general(
            queries[b, 0], held_keys[b], (((0,), (0,)), ((), ())), preferred_element_type=jnp.float32
        )
        scores = scores * DH ** (-0.5)
        offset = jnp.full((ROWS, 1), offsets[b, 0], jnp.int32)
        for j in range(1, DRAFT):
            offset = jnp.where(draft == j, offsets[b, j], offset)
        seen = positions < lengths[b] - offset
        scores = jnp.where(seen, scores, masked_score)
        block_max = jnp.max(scores, axis=1, keepdims=True)
        weights = jnp.where(seen, jnp.exp(scores - block_max), 0.0)
        block_sum = jnp.sum(weights, axis=1, keepdims=True)
        value_copy(b).wait()
        block_out = lax.dot_general(
            weights.astype(jnp.bfloat16),
            held_values[b],
            (((1,), (1,)), ((), ())),
            preferred_element_type=jnp.float32,
        )
        out[pl.ds(b * ROWS, ROWS), 0, :] = block_out
        out[pl.ds(b * ROWS, ROWS), 1, :] = jnp.where(lane < LANES // 2, block_max, block_sum)


def merge_pair(parts, out):
    lane = lax.broadcasted_iota(jnp.int32, (HALF, LANES), 1)
    stats = [parts[c, :, 1, :] for c in range(CORES)]
    tops = [s[:, :1] for s in stats]
    top = jnp.maximum(tops[0], tops[1])
    factors = [jnp.exp(t - top) for t in tops]
    total = sum(f * s[:, LANES // 2 : LANES // 2 + 1] for f, s in zip(factors, stats))
    out[:, 0, :] = sum(f * parts[c, :, 0, :] for c, f in enumerate(factors))
    out[:, 1, :] = jnp.where(lane < LANES // 2, top, total)


def merge_chips(parts, out):
    stats = parts[:, 1, :]
    tops = stats[:, :1]
    factor = jnp.exp(tops - jnp.max(tops, axis=0, keepdims=True))
    total = jnp.sum(factor * stats[:, LANES // 2 : LANES // 2 + 1], axis=0, keepdims=True)
    summed = jnp.sum(factor * parts[:, 0, :], axis=0, keepdims=True)
    out[...] = jnp.broadcast_to((summed / total)[None], out.shape)


def project(attended, out_proj, out):
    total = jnp.zeros((BATCH * DRAFT, COLS), jnp.float32)
    for h in range(HEADS):
        rows = attended[pl.ds(h, BATCH * DRAFT, stride=HEADS), :].astype(jnp.bfloat16)
        total += jnp.dot(rows, out_proj[0, h], preferred_element_type=jnp.float32)
    out[...] = total.reshape(BATCH, DRAFT, COLS)


def shards(queries, keys, values, lengths, offsets, out_proj):
    f32 = jnp.float32
    block = pl.pallas_call(
        attend_block,
        out_shape=jax.ShapeDtypeStruct((CORES * HALF, 2, LANES), f32),
        in_specs=[smem, smem, vmem, hbm, hbm],
        out_specs=vmem,
        scratch_shapes=[
            pltpu.VMEM((BATCH, DH, CTX_DEV), jnp.bfloat16),
            pltpu.VMEM((BATCH, DH, CTX_DEV), jnp.bfloat16),
            pltpu.SemaphoreType.DMA((BATCH,)),
            pltpu.SemaphoreType.DMA((BATCH,)),
        ],
        compiler_params=pltpu.CompilerParams(vmem_limit_bytes=16 * 2**20),
        name="attend_block",
    )(lengths, offsets, queries, keys, values)
    pair = lax.all_to_all(block.reshape(CORES, HALF, 2, LANES), "core", 0, 0, tiled=True)
    chip = pl.pallas_call(
        merge_pair,
        out_shape=jax.ShapeDtypeStruct((HALF, 2, LANES), f32),
        in_specs=[vmem],
        out_specs=vmem,
        name="merge_pair",
    )(pair)
    parts = lax.all_to_all(chip, ("y", "z"), 0, 0, tiled=True)
    copies = pl.pallas_call(
        merge_chips,
        out_shape=jax.ShapeDtypeStruct((CHIPS, 1, LANES), f32),
        in_specs=[vmem],
        out_specs=vmem,
        name="merge_chips",
    )(parts)
    rows = lax.all_to_all(copies, ("y", "z"), 0, 0, tiled=True)
    attended = lax.all_gather(rows, "core", axis=0, tiled=True).reshape(CORES * HALF, LANES)
    partial_out = pl.pallas_call(
        project,
        out_shape=jax.ShapeDtypeStruct((BATCH, DRAFT, COLS), f32),
        in_specs=[vmem, vmem],
        out_specs=vmem,
        name="project",
    )(attended, out_proj)
    return lax.psum(partial_out, "head")


def solution(mesh):
    fine = Mesh(mesh.devices.reshape(Y, Z, CORES, HEAD), ("y", "z", "core", "head"))
    seq = ("y", "z", "core")
    placed = (
        P(None, "head", None, None),
        P(None, "head", None, seq),
        P(None, "head", None, seq),
        P(),
        P(),
        P("head", None, None, seq),
    )
    return jax.shard_map(
        shards, mesh=fine, in_specs=placed, out_specs=P(None, None, seq), check_vma=False
    )
```

time: 585 us -> 82.6 us (0.14)
  blocking collectives: 515 us -> 51.3 us
  waiting for transfers between devices: 51.7 us -> 12.4 us
  between operations: 13.4 us -> 0.06 us
  Pallas kernels: 0 us -> 8.88 us
    pmax x1 -> x0, blocking collectives: 255 us -> none  [shards(): row_top = lax.pmax(block_max, 'seq')]
    psum x1 -> x0, blocking collectives: 251 us -> none  [shards(): lax.psum((block_sum * factor, block_out * factor[..., None]), 'seq')]
    psum x1 -> x0, waiting for transfers between devices: 51.6 us -> none  [shards(): lax.psum((block_sum * factor, block_out * factor[..., None]), 'seq')]
    all_to_all x0 -> x2, blocking collectives: none -> 37.9 us  [the longest x1 26.8 us: shards(): parts = lax.all_to_all(chip, ('y', 'z'), 0, 0, tiled=True)]
    all_to_all x0 -> x1, waiting for transfers between devices: none -> 12.4 us  [shards(): rows = lax.all_to_all(copies, ('y', 'z'), 0, 0, tiled=True)]
    pallas_call x0 -> x4, Pallas kernels: none -> 8.88 us  [the longest x1 3.44 us: shards(): pl.pallas_call(attend_block, out_shape=jax.ShapeDtypeStruct((CORES * HALF...]
  transfers between devices with their start and end apart: 1 -> 1, of which waited for: 1 -> 1; matrix products, arithmetic and copies ran while one was open for 0% -> 1% of each run, Pallas kernels for 0% -> 0%
where the time goes in v1:
time: 82.6 us; the launch traced here: 82.1 us
  blocking collectives  51.3 us (62%)
  waiting for transfers between devices  12.4 us (15%)
  Pallas kernels  8.88 us (11%)
  starting transfers between devices  5.25 us (6%)
  local copies, waits for them, and re-layouts  4.2 us (5%)
    all_to_all x1, blocking collectives, shards(): parts = lax.all_to_all(chip, ('y', 'z'), 0, 0, tiled=True)  26.8 us
    all_to_all x1, waiting for transfers between devices, shards(): rows = lax.all_to_all(copies, ('y', 'z'), 0, 0, tiled=True)  12.4 us
    all_to_all x1, blocking collectives, shards(): lax.all_to_all(block.reshape(CORES, HALF, 2, LANES), 'core', 0, 0, tiled=...  11.1 us
    psum x1, blocking collectives, shards(): return lax.psum(partial_out, 'head')  9.26 us
    all_to_all x1, starting transfers between devices, shards(): rows = lax.all_to_all(copies, ('y', 'z'), 0, 0, tiled=True)  5.25 us
    unnamed x12, local copies, waits for them, and re-layouts  4.2 us
    all_gather x1, blocking collectives, shards(): lax.all_gather(rows, 'core', axis=0, tiled=True)  4.14 us
    pallas_call x1, Pallas kernels, shards(): pl.pallas_call(attend_block, out_shape=jax.ShapeDtypeStruct((CORES * HALF...  3.44 us
  transfers between devices with their start and end apart: 1, of which 1 were waited for; matrix products, arithmetic and copies ran while one was open for 1% of the time, Pallas kernels for 0%

profile of v1, /device:TPU:1, one launch (start us, length us, event | category | flops | bytes accessed | tf_op | source)
XLA Modules:
  0.0 82.1 jit_solution(4631437199550716366)
XLA Ops:
  0.0 0.0 copy-start.2
  0.0 0.0 copy-start.3
  0.0 0.9 %copy.10.queries = bf16[4,1,128,32]{3,2,1,0:T(8,128)(2,1)S(1)} copy(bf16[4,1,128,32]{2,3,1,0:T(8,128)(2,1)} %param.6) | data formatting | bytes 65536 | tf_op args[0]
  0.9 0.0 copy-done.2
  0.9 0.0 copy-done.3
  0.9 0.0 copy-start
  0.9 1.2 %copy-done = bf16[4,1,128,1024]{3,2,1,0:T(8,128)(2,1)S(1)} copy-done((bf16[4,1,128,1024]{3,2,1,0:T(8,128)(2,1)S(1)}, bf16[4,1,128,1024]{3,2,1,0:T(8,128)(2,1)}, u32[]{:S(2)}) %copy-start) | copy-done | bytes 1048600
  2.2 0.0 copy-start.1
  2.2 1.2 %copy-done.1 = bf16[4,1,128,1024]{3,2,1,0:T(8,128)(2,1)S(1)} copy-done((bf16[4,1,128,1024]{3,2,1,0:T(8,128)(2,1)S(1)}, bf16[4,1,128,1024]{3,2,1,0:T(8,128)(2,1)}, u32[]{:S(2)}) %copy-start.1) | copy-done | bytes 1048600
  3.4 3.4 %attend_block.1 = f32[128,2,128]{2,1,0:T(2,128)S(1)} custom-call(s32[4]{0:T(128)S(1)} %copy-done.3, s32[4,4]{1,0:T(4,128)S(1)} %copy-done.2, bf16[4,1,128,32]{3,2,1,0:T(8,128)(2,1)S(1)} %copy.10.queries, bf16[4,1,128,1024]{3,2,1,0:T(8,128)(2,1)S(1)} %copy-done, bf16[4,1,128,1024]{3,2,1,0:T(8,128)(2,1)S(1)} %copy-done.1), custom_call_target="tpu_custom_call" | custom-call | tf_op jit(solution)/shard_map/attend_block/pallas_call | solution.py:88
  6.8 11.1 %all_to_all.15.parts = f32[2,64,2,128]{3,2,1,0:T(2,128)} all-to-all(f32[2,64,2,128]{3,2,1,0:T(2,128)S(1)} %bitcast.3), channel_id=1, replica_groups=mesh['y'=4,'z'=16,'core'=2,'head'=4] {'core'}, dimensions={0} | all-to-all | bytes 262144 | tf_op jit(solution)/shard_map/all_to_all | solution.py:102
  17.9 2.0 %merge_pair.1 = f32[64,2,128]{2,1,0:T(2,128)} custom-call(f32[2,64,2,128]{3,2,1,0:T(2,128)} %all_to_all.15.parts), custom_call_target="tpu_custom_call" | custom-call | tf_op jit(solution)/shard_map/merge_pair/pallas_call | solution.py:103
  19.9 0.0 copy-start.4
  19.9 26.8 %all_to_all.16.parts = f32[64,2,128]{2,1,0:T(2,128)} all-to-all(f32[64,2,128]{2,1,0:T(2,128)} %merge_pair.1), channel_id=1, replica_groups=mesh['y'=4,'z'=16,'core'=2,'head'=4] {'y','z'}, dimensions={0} | all-to-all | bytes 131072 | tf_op jit(solution)/shard_map/all_to_all | solution.py:110
  46.7 1.7 %merge_chips.1 = f32[64,1,128]{2,1,0:T(1,128)} custom-call(f32[64,2,128]{2,1,0:T(2,128)} %all_to_all.16.parts), custom_call_target="tpu_custom_call" | custom-call | tf_op jit(solution)/shard_map/merge_chips/pallas_call | solution.py:111
  48.4 5.3 %all-to-all-start.2 = ((f32[64,1,128]{2,1,0:T(1,128)}), f32[64,1,128]{2,1,0:T(1,128)S(1)}, u32[]{:S(2)}, u32[]{:S(2)}) async-start(f32[64,1,128]{2,1,0:T(1,128)} %merge_chips.1), calls=%async_computation.2 | async-start | bytes 65536 | tf_op jit(solution)/shard_map/all_to_all | solution.py:118
  53.7 0.0 copy-done.4
  53.7 0.8 %copy.12.out_proj = bf16[1,8,128,64]{3,2,1,0:T(8,128)(2,1)} copy(bf16[1,8,128,64]{2,3,1,0:T(8,128)(2,1)S(1)} %copy-done.4) | data formatting | bytes 262144 | tf_op args[5]
  54.5 12.4 %all-to-all-done.2 = f32[64,1,128]{2,1,0:T(1,128)S(1)} async-done(((f32[64,1,128]{2,1,0:T(1,128)}), f32[64,1,128]{2,1,0:T(1,128)S(1)}, u32[]{:S(2)}, u32[]{:S(2)}) %all-to-all-start.2) | async-done | bytes 32800 | tf_op jit(solution)/shard_map/all_to_all | solution.py:118
  66.9 4.1 %all_gather.3 = f32[128,1,128]{2,0,1:T(8,128)} all-gather(f32[64,1,128]{2,0,1:T(8,128)S(1)} %bitcast.5), channel_id=1, replica_groups=mesh['y'=4,'z'=16,'core'=2,'head'=4] {'core'}, dimensions={0}, use_global_device_ids=true | all-gather | bytes 98304 | tf_op jit(solution)/shard_map/all_gather | solution.py:119
  71.1 1.8 %project.1 = f32[4,4,64]{2,1,0:T(4,128)} custom-call(f32[128,128]{1,0:T(8,128)} %bitcast.4, bf16[1,8,128,64]{3,2,1,0:T(8,128)(2,1)} %copy.12.out_proj), custom_call_target="tpu_custom_call" | custom-call | tf_op jit(solution)/shard_map/project/pallas_call | solution.py:120
  72.8 9.3 %psum.7 = f32[4,4,64]{2,1,0:T(4,128)} all-reduce(f32[4,4,64]{2,1,0:T(4,128)} %project.1), channel_id=1, replica_groups=mesh['y'=4,'z'=16,'core'=2,'head'=4] {'head'}, use_global_device_ids=true, to_apply=%region_0.0 | all-reduce | flops 1024 | bytes 8192 | tf_op jit(solution)/shard_map/psum | solution.py:127
Async XLA Ops:
  0.0 0.9 %copy-start.2 = (s32[4,4]{1,0:T(4,128)S(1)}, s32[4,4]{1,0:T(4,128)}, u32[]{:S(2)}) copy-start(s32[4,4]{1,0:T(4,128)} %offsets.1) | copy-start | bytes 196
  0.0 0.9 %copy-start.3 = (s32[4]{0:T(128)S(1)}, s32[4]{0:T(128)}, u32[]{:S(2)}) copy-start(s32[4]{0:T(128)} %lengths.1) | copy-start | bytes 52
  0.9 1.2 %copy-start = (bf16[4,1,128,1024]{3,2,1,0:T(8,128)(2,1)S(1)}, bf16[4,1,128,1024]{3,2,1,0:T(8,128)(2,1)}, u32[]{:S(2)}) copy-start(bf16[4,1,128,1024]{3,2,1,0:T(8,128)(2,1)} %keys.1) | copy-start | bytes 3145732
  2.2 1.2 %copy-start.1 = (bf16[4,1,128,1024]{3,2,1,0:T(8,128)(2,1)S(1)}, bf16[4,1,128,1024]{3,2,1,0:T(8,128)(2,1)}, u32[]{:S(2)}) copy-start(bf16[4,1,128,1024]{3,2,1,0:T(8,128)(2,1)} %values.1) | copy-start | bytes 3145732
  19.9 33.7 %copy-start.4 = (bf16[1,8,128,64]{2,3,1,0:T(8,128)(2,1)S(1)}, bf16[1,8,128,64]{2,3,1,0:T(8,128)(2,1)}, u32[]{:S(2)}) copy-start(bf16[1,8,128,64]{2,3,1,0:T(8,128)(2,1)} %param.11) | copy-start | bytes 393220
  48.4 18.5 %all-to-all-start.2 = ((f32[64,1,128]{2,1,0:T(1,128)}), f32[64,1,128]{2,1,0:T(1,128)S(1)}, u32[]{:S(2)}, u32[]{:S(2)}) async-start(f32[64,1,128]{2,1,0:T(1,128)} %merge_chips.1), calls=%async_computation.2 | async-start | bytes 65536 | tf_op jit(solution)/shard_map/all_to_all | solution.py:118

commit v2 on v1

v2 whole, which is shorter than its diff:
```python
import jax
import jax.numpy as jnp
from jax import lax
from jax.experimental import pallas as pl
from jax.experimental.pallas import tpu as pltpu
from jax.sharding import Mesh, PartitionSpec as P

masked_score = -1e30
Y, FAR, NEAR, CORES, HEAD = 4, 8, 2, 2, 4
BATCH, DRAFT, HEADS, ROWS, DH, CTX_DEV, COLS = 4, 4, 8, 32, 128, 1024, 64
TOKENS = BATCH * DRAFT
LANES = 128
near_axes = ("y", "near", "core")
vmem = pl.BlockSpec(memory_space=pltpu.VMEM)
smem = pl.BlockSpec(memory_space=pltpu.SMEM)
hbm = pl.BlockSpec(memory_space=pl.ANY)


def pack_stats(top, total):
    lane = lax.broadcasted_iota(jnp.int32, top.shape[:-1] + (LANES,), top.ndim - 1)
    return jnp.where(lane < LANES // 2, top, total)


def merge(parts):
    stats = parts[:, HEADS:, :]
    tops = stats[:, :, :1]
    top = jnp.max(tops, axis=0)
    factor = jnp.exp(tops - top[None])
    total = jnp.sum(factor * stats[:, :, LANES // 2 : LANES // 2 + 1], axis=0)
    summed = jnp.sum(factor * parts[:, :HEADS, :], axis=0)
    return top, total, summed


def attend_block(lengths, offsets, queries, keys, values, out, held_keys, held_values, key_sems, value_sems):
    def key_copy(b):
        return pltpu.make_async_copy(keys.at[b, 0], held_keys.at[b], key_sems.at[b])

    def value_copy(b):
        return pltpu.make_async_copy(values.at[b, 0], held_values.at[b], value_sems.at[b])

    for b in range(BATCH):
        key_copy(b).start()
        value_copy(b).start()
    chip = (lax.axis_index("y") * FAR + lax.axis_index("far")) * NEAR + lax.axis_index("near")
    index = chip * CORES + lax.axis_index("core")
    positions = index * CTX_DEV + lax.broadcasted_iota(jnp.int32, (ROWS, CTX_DEV), 1)
    draft = lax.broadcasted_iota(jnp.int32, (ROWS, 1), 0) // HEADS
    for b in range(BATCH):
        key_copy(b).wait()
        scores = jnp.dot(queries[b, 0], held_keys[b], preferred_element_type=jnp.float32)
        scores = scores * DH ** (-0.5)
        offset = jnp.full((ROWS, 1), offsets[b, 0], jnp.int32)
        for j in range(1, DRAFT):
            offset = jnp.where(draft == j, offsets[b, j], offset)
        seen = positions < lengths[b] - offset
        scores = jnp.where(seen, scores, masked_score)
        block_max = jnp.max(scores, axis=1, keepdims=True)
        weights = jnp.where(seen, jnp.exp(scores - block_max), 0.0)
        block_sum = jnp.sum(weights, axis=1, keepdims=True)
        value_copy(b).wait()
        block_out = lax.dot_general(
            weights.astype(jnp.bfloat16),
            held_values[b],
            (((1,), (1,)), ((), ())),
            preferred_element_type=jnp.float32,
        )
        tokens = pl.ds(b * DRAFT, DRAFT)
        out[tokens, :HEADS, :] = block_out.reshape(DRAFT, HEADS, LANES)
        out[tokens, HEADS:, :] = pack_stats(block_max, block_sum).reshape(DRAFT, HEADS, LANES)


def merge_near(parts, out):
    top, total, summed = merge(parts)
    out[:, :HEADS, :] = jnp.broadcast_to(summed[None], (FAR, HEADS, LANES))
    out[:, HEADS:, :] = jnp.broadcast_to(pack_stats(top, total)[None], (FAR, HEADS, LANES))


def merge_far(parts, out):
    _, total, summed = merge(parts)
    out[...] = jnp.broadcast_to((summed / total)[None], out.shape)


def project(attended, out_proj, out):
    total = jnp.zeros((TOKENS, COLS), jnp.float32)
    for h in range(HEADS):
        rows = attended[pl.ds(h, TOKENS, stride=HEADS), :].astype(jnp.bfloat16)
        total += lax.dot_general(
            rows, out_proj[0, h], (((1,), (1,)), ((), ())), preferred_element_type=jnp.float32
        )
    out[...] = total.reshape(BATCH, DRAFT, COLS)


def shards(queries, keys, values, lengths, offsets, out_proj):
    def packed(copies, rows):
        return jax.ShapeDtypeStruct((copies, rows, LANES), jnp.float32)

    block = pl.pallas_call(
        attend_block,
        out_shape=packed(TOKENS, 2 * HEADS),
        in_specs=[smem, smem, vmem, hbm, hbm],
        out_specs=vmem,
        scratch_shapes=[
            pltpu.VMEM((BATCH, DH, CTX_DEV), jnp.bfloat16),
            pltpu.VMEM((BATCH, DH, CTX_DEV), jnp.bfloat16),
            pltpu.SemaphoreType.DMA((BATCH,)),
            pltpu.SemaphoreType.DMA((BATCH,)),
        ],
        name="attend_block",
    )(lengths, offsets, queries.swapaxes(2, 3), keys, values)
    parts = lax.all_to_all(block, near_axes, 0, 0, tiled=True)
    copies = pl.pallas_call(
        merge_near, out_shape=packed(FAR, 2 * HEADS), in_specs=[vmem], out_specs=vmem, name="merge_near"
    )(parts)
    parts = lax.all_to_all(copies, "far", 0, 0, tiled=True)
    copies = pl.pallas_call(
        merge_far, out_shape=packed(TOKENS, HEADS), in_specs=[vmem], out_specs=vmem, name="merge_far"
    )(parts)
    rows = lax.all_to_all(copies, near_axes, 0, 0, tiled=True)
    partial_out = pl.pallas_call(
        project,
        out_shape=jax.ShapeDtypeStruct((BATCH, DRAFT, COLS), jnp.float32),
        in_specs=[vmem, vmem],
        out_specs=vmem,
        name="project",
    )(rows.reshape(TOKENS * HEADS, LANES), out_proj.swapaxes(2, 3))
    return lax.psum(partial_out, "head")


def solution(mesh):
    fine = Mesh(
        mesh.devices.reshape(Y, FAR, NEAR, CORES, HEAD), ("y", "far", "near", "core", "head")
    )
    seq = ("y", "far", "near", "core")
    placed = (
        P(None, "head", None, None),
        P(None, "head", None, seq),
        P(None, "head", None, seq),
        P(),
        P(),
        P("head", None, None, seq),
    )
    return jax.shard_map(
        shards, mesh=fine, in_specs=placed, out_specs=P(None, None, seq), check_vma=False
    )
```

time: 82.6 us -> 71.6 us (0.87)
  waiting for transfers between devices: 12.4 us -> 0 us
  blocking collectives: 51.3 us -> 61.2 us
  starting transfers between devices: 5.25 us -> 0 us
  local copies, waits for them, and re-layouts: 4.2 us -> 0 us
  Pallas kernels: 8.88 us -> 9.91 us
    all_to_all x2 -> x3, blocking collectives: 37.9 us -> 51.9 us  [the longest x1 22.7 us: shards(): parts = lax.all_to_all(copies, 'far', 0, 0, tiled=True)]
    all_to_all x1 -> x0, waiting for transfers between devices: 12.4 us -> none  [shards(): rows = lax.all_to_all(copies, ('y', 'z'), 0, 0, tiled=True)]
    all_to_all x1 -> x0, starting transfers between devices: 5.25 us -> none  [shards(): rows = lax.all_to_all(copies, ('y', 'z'), 0, 0, tiled=True)]
    unnamed x12 -> x0, local copies, waits for them, and re-layouts: 4.2 us -> none
    all_gather x1 -> x0, blocking collectives: 4.14 us -> none  [shards(): lax.all_gather(rows, 'core', axis=0, tiled=True)]
    pallas_call x3, Pallas kernels: 7.11 us -> 8.18 us  [the longest x1 4.89 us: shards(): pl.pallas_call(attend_block, out_shape=packed(TOKENS, 2 * HEADS), in_spec...]
  transfers between devices with their start and end apart: 1 -> 0, of which waited for: 1 -> 0; matrix products, arithmetic and copies ran while one was open for 1% -> 0% of each run, Pallas kernels for 0% -> 0%
where the time goes in v2:
time: 71.6 us; the launch traced here: 71.1 us
  blocking collectives  61.2 us (85%)
  Pallas kernels  9.91 us (14%)
    all_to_all x1, blocking collectives, shards(): parts = lax.all_to_all(copies, 'far', 0, 0, tiled=True)  22.7 us
    all_to_all x1, blocking collectives, shards(): parts = lax.all_to_all(block, near_axes, 0, 0, tiled=True)  17.1 us
    all_to_all x1, blocking collectives, shards(): rows = lax.all_to_all(copies, near_axes, 0, 0, tiled=True)  12.1 us
    psum x1, blocking collectives, shards(): return lax.psum(partial_out, 'head')  9.26 us
    pallas_call x1, Pallas kernels, shards(): pl.pallas_call(attend_block, out_shape=packed(TOKENS, 2 * HEADS), in_spec...  4.89 us
    pallas_call x1, Pallas kernels, shards(): pl.pallas_call(project, out_shape=jax.ShapeDtypeStruct((BATCH, DRAFT, COL...  1.73 us
    pallas_call x1, Pallas kernels, shards(): pl.pallas_call(merge_near, out_shape=packed(FAR, 2 * HEADS), in_specs=[vm...  1.68 us
    pallas_call x1, Pallas kernels, shards(): pl.pallas_call(merge_far, out_shape=packed(TOKENS, HEADS), in_specs=[vmem...  1.62 us

profile of v2, /device:TPU:1, one launch (start us, length us, event | category | flops | bytes accessed | tf_op | source)
XLA Modules:
  0.0 71.1 jit_solution(1565530090224352674)
XLA Ops:
  0.0 4.9 %attend_block.1 = f32[16,16,128]{2,1,0:T(8,128)} custom-call(s32[4]{0:T(128)} %lengths.1, s32[4,4]{1,0:T(4,128)} %offsets.1, bf16[4,1,32,128]{3,2,1,0:T(8,128)(2,1)} %bitcast.5, bf16[4,1,128,1024]{3,2,1,0:T(8,128)(2,1)} %keys.1, bf16[4,1,128,1024]{3,2,1,0:T(8,128)(2,1)} %values.1), custom_call_target="tpu_custom_call" | custom-call | tf_op jit(solution)/shard_map/attend_block/pallas_call | solution.py:97
  4.9 17.1 %all_to_all.15.parts = f32[16,16,128]{2,1,0:T(8,128)} all-to-all(f32[16,16,128]{2,1,0:T(8,128)} %attend_block.1), channel_id=1, replica_groups=mesh['y'=4,'far'=8,'near'=2,'core'=2,'head'=4] {'y','near','core'}, dimensions={0} | all-to-all | bytes 262144 | tf_op jit(solution)/shard_map/all_to_all | solution.py:110
  22.0 1.7 %merge_near.1 = f32[8,16,128]{2,1,0:T(8,128)} custom-call(f32[16,16,128]{2,1,0:T(8,128)} %all_to_all.15.parts), custom_call_target="tpu_custom_call" | custom-call | tf_op jit(solution)/shard_map/merge_near/pallas_call | solution.py:111
  23.7 22.7 %all_to_all.16.parts = f32[8,16,128]{2,1,0:T(8,128)} all-to-all(f32[8,16,128]{2,1,0:T(8,128)} %merge_near.1), channel_id=1, replica_groups=mesh['y'=4,'far'=8,'near'=2,'core'=2,'head'=4] {'far'}, dimensions={0} | all-to-all | bytes 131072 | tf_op jit(solution)/shard_map/all_to_all | solution.py:114
  46.4 1.6 %merge_far.1 = f32[16,8,128]{2,1,0:T(8,128)} custom-call(f32[8,16,128]{2,1,0:T(8,128)} %all_to_all.16.parts), custom_call_target="tpu_custom_call" | custom-call | tf_op jit(solution)/shard_map/merge_far/pallas_call | solution.py:115
  48.0 12.1 %all_to_all.17 = f32[16,8,128]{2,1,0:T(8,128)} all-to-all(f32[16,8,128]{2,1,0:T(8,128)} %merge_far.1), channel_id=1, replica_groups=mesh['y'=4,'far'=8,'near'=2,'core'=2,'head'=4] {'y','near','core'}, dimensions={0} | all-to-all | bytes 131072 | tf_op jit(solution)/shard_map/all_to_all | solution.py:118
  60.1 1.7 %project.1 = f32[4,4,64]{2,1,0:T(4,128)} custom-call(f32[128,128]{1,0:T(8,128)} %bitcast.3, bf16[1,8,64,128]{3,2,1,0:T(8,128)(2,1)} %bitcast.4), custom_call_target="tpu_custom_call" | custom-call | tf_op jit(solution)/shard_map/project/pallas_call | solution.py:119
  61.8 9.3 %psum.7 = f32[4,4,64]{2,1,0:T(4,128)} all-reduce(f32[4,4,64]{2,1,0:T(4,128)} %project.1), channel_id=1, replica_groups=mesh['y'=4,'far'=8,'near'=2,'core'=2,'head'=4] {'head'}, use_global_device_ids=true, to_apply=%region_0.0 | all-reduce | flops 1024 | bytes 8192 | tf_op jit(solution)/shard_map/psum | solution.py:126

commit v3 on v2

--- a/solution.py
+++ b/solution.py
@@ -12,8 +12,13 @@
 LANES = 128
 near_axes = ("y", "near", "core")
 vmem = pl.BlockSpec(memory_space=pltpu.VMEM)
-smem = pl.BlockSpec(memory_space=pltpu.SMEM)
-hbm = pl.BlockSpec(memory_space=pl.ANY)
+hbm = pl.BlockSpec(memory_space=pltpu.HBM)
+attend_params = pltpu.CompilerParams(vmem_limit_bytes=8 * 2**20)
+small_params = pltpu.CompilerParams(vmem_limit_bytes=2 * 2**20)
+
+
+def in_hbm(x):
+    return pltpu.with_memory_space_constraint(x, pltpu.HBM)
 
 
 def pack_stats(top, total):
@@ -31,42 +36,52 @@
     return top, total, summed
 
 
-def attend_block(lengths, offsets, queries, keys, values, out, held_keys, held_values, key_sems, value_sems):
-    def key_copy(b):
-        return pltpu.make_async_copy(keys.at[b, 0], held_keys.at[b], key_sems.at[b])
-
-    def value_copy(b):
-        return pltpu.make_async_copy(values.at[b, 0], held_values.at[b], value_sems.at[b])
-
-    for b in range(BATCH):
-        key_copy(b).start()
-        value_copy(b).start()
+def attend_block(lengths, offsets, queries, keys, values, out, *scratch):
+    held_lengths, held_offsets, held_queries, held_keys, held_values, small_sems, key_sems, value_sems = scratch
+    small = [
+        pltpu.make_async_copy(source, target, small_sems.at[i])
+        for i, (source, target) in enumerate(
+            ((queries, held_queries), (lengths, held_lengths), (offsets, held_offsets))
+        )
+    ]
+    key_copies = [
+        pltpu.make_async_copy(keys.at[b, 0], held_keys.at[b], key_sems.at[b]) for b in range(BATCH)
+    ]
+    value_copies = [
+        pltpu.make_async_copy(values.at[b, 0], held_values.at[b], value_sems.at[b])
+        for b in range(BATCH)
+    ]
+    for copy in small + key_copies + value_copies:
+        copy.start()
     chip = (lax.axis_index("y") * FAR + lax.axis_index("far")) * NEAR + lax.axis_index("near")
     index = chip * CORES + lax.axis_index("core")
     positions = index * CTX_DEV + lax.broadcasted_iota(jnp.int32, (ROWS, CTX_DEV), 1)
     draft = lax.broadcasted_iota(jnp.int32, (ROWS, 1), 0) // HEADS
+    for copy in small:
+        copy.wait()
+    weights = []
     for b in range(BATCH):
-        key_copy(b).wait()
-        scores = jnp.dot(queries[b, 0], held_keys[b], preferred_element_type=jnp.float32)
+        key_copies[b].wait()
+        scores = jnp.dot(held_queries[b, 0], held_keys[b], preferred_element_type=jnp.float32)
         scores = scores * DH ** (-0.5)
-        offset = jnp.full((ROWS, 1), offsets[b, 0], jnp.int32)
+        offset = jnp.full((ROWS, 1), held_offsets[b, 0], jnp.int32)
         for j in range(1, DRAFT):
-            offset = jnp.where(draft == j, offsets[b, j], offset)
-        seen = positions < lengths[b] - offset
+            offset = jnp.where(draft == j, held_offsets[b, j], offset)
+        seen = positions < held_lengths[b] - offset
         scores = jnp.where(seen, scores, masked_score)
         block_max = jnp.max(scores, axis=1, keepdims=True)
-        weights = jnp.where(seen, jnp.exp(scores - block_max), 0.0)
-        block_sum = jnp.sum(weights, axis=1, keepdims=True)
-        value_copy(b).wait()
+        weight = jnp.where(seen, jnp.exp(scores - block_max), 0.0)
+        block_sum = jnp.sum(weight, axis=1, keepdims=True)
+        weights.append(weight.astype(jnp.bfloat16))
+        out[pl.ds(b * DRAFT, DRAFT), HEADS:, :] = pack_stats(block_max, block_sum).reshape(
+            DRAFT, HEADS, LANES
+        )
+    for b in range(BATCH):
+        value_copies[b].wait()
         block_out = lax.dot_general(
-            weights.astype(jnp.bfloat16),
-            held_values[b],
-            (((1,), (1,)), ((), ())),
-            preferred_element_type=jnp.float32,
+            weights[b], held_values[b], (((1,), (1,)), ((), ())), preferred_element_type=jnp.float32
         )
-        tokens = pl.ds(b * DRAFT, DRAFT)
-        out[tokens, :HEADS, :] = block_out.reshape(DRAFT, HEADS, LANES)
-        out[tokens, HEADS:, :] = pack_stats(block_max, block_sum).reshape(DRAFT, HEADS, LANES)
+        out[pl.ds(b * DRAFT, DRAFT), :HEADS, :] = block_out.reshape(DRAFT, HEADS, LANES)
 
 
 def merge_near(parts, out):
@@ -97,23 +112,30 @@
     block = pl.pallas_call(
         attend_block,
         out_shape=packed(TOKENS, 2 * HEADS),
-        in_specs=[smem, smem, vmem, hbm, hbm],
+        in_specs=[hbm] * 5,
         out_specs=vmem,
         scratch_shapes=[
+            pltpu.SMEM((BATCH,), jnp.int32),
+            pltpu.SMEM((BATCH, DRAFT), jnp.int32),
+            pltpu.VMEM((BATCH, 1, ROWS, DH), jnp.bfloat16),
             pltpu.VMEM((BATCH, DH, CTX_DEV), jnp.bfloat16),
             pltpu.VMEM((BATCH, DH, CTX_DEV), jnp.bfloat16),
+            pltpu.SemaphoreType.DMA((3,)),
             pltpu.SemaphoreType.DMA((BATCH,)),
             pltpu.SemaphoreType.DMA((BATCH,)),
         ],
+        compiler_params=attend_params,
         name="attend_block",
-    )(lengths, offsets, queries.swapaxes(2, 3), keys, values)
+    )(*(in_hbm(x) for x in (lengths, offsets, queries.swapaxes(2, 3), keys, values)))
     parts = lax.all_to_all(block, near_axes, 0, 0, tiled=True)
     copies = pl.pallas_call(
-        merge_near, out_shape=packed(FAR, 2 * HEADS), in_specs=[vmem], out_specs=vmem, name="merge_near"
+        merge_near, out_shape=packed(FAR, 2 * HEADS), in_specs=[vmem], out_specs=vmem,
+        compiler_params=small_params, name="merge_near"
     )(parts)
     parts = lax.all_to_all(copies, "far", 0, 0, tiled=True)
     copies = pl.pallas_call(
-        merge_far, out_shape=packed(TOKENS, HEADS), in_specs=[vmem], out_specs=vmem, name="merge_far"
+        merge_far, out_shape=packed(TOKENS, HEADS), in_specs=[vmem], out_specs=vmem,
+        compiler_params=small_params, name="merge_far"
     )(parts)
     rows = lax.all_to_all(copies, near_axes, 0, 0, tiled=True)
     partial_out = pl.pallas_call(
@@ -121,6 +143,7 @@
         out_shape=jax.ShapeDtypeStruct((BATCH, DRAFT, COLS), jnp.float32),
         in_specs=[vmem, vmem],
         out_specs=vmem,
+        compiler_params=small_params,
         name="project",
     )(rows.reshape(TOKENS * HEADS, LANES), out_proj.swapaxes(2, 3))
     return lax.psum(partial_out, "head")

time: 71.6 us -> 63.3 us (0.88)
  Pallas kernels: 9.91 us -> 3.94 us
  blocking collectives: 61.2 us -> 59.1 us
    all_to_all x1, blocking collectives: 17.1 us -> 15.5 us  [shards(): parts = lax.all_to_all(block, near_axes, 0, 0, tiled=True)]
    pallas_call x1, Pallas kernels: 1.73 us -> 0.17 us  [shards(): pl.pallas_call(project, out_shape=jax.ShapeDtypeStruct((BATCH, DRAFT, COL...]
    pallas_call x1, Pallas kernels: 1.68 us -> 0.15 us  [shards(): pl.pallas_call(merge_near, out_shape=packed(FAR, 2 * HEADS), in_specs=[vm...]
    pallas_call x1, Pallas kernels: 1.62 us -> 0.16 us  [shards(): pl.pallas_call(merge_far, out_shape=packed(TOKENS, HEADS), in_specs=[vmem...]
    pallas_call x1, Pallas kernels: 4.89 us -> 3.46 us  [shards(): pl.pallas_call(attend_block, out_shape=packed(TOKENS, 2 * HEADS), in_spec...]
    all_to_all x1, blocking collectives: 12.1 us -> 10.8 us  [shards(): rows = lax.all_to_all(copies, near_axes, 0, 0, tiled=True)]
    all_to_all x1, blocking collectives: 22.7 us -> 23.7 us  [shards(): parts = lax.all_to_all(copies, 'far', 0, 0, tiled=True)]
where the time goes in v3:
time: 63.3 us; the launch traced here: 63.1 us
  blocking collectives  59.1 us (93%)
  Pallas kernels  3.94 us (6%)
    all_to_all x1, blocking collectives, shards(): parts = lax.all_to_all(copies, 'far', 0, 0, tiled=True)  23.7 us
    all_to_all x1, blocking collectives, shards(): parts = lax.all_to_all(block, near_axes, 0, 0, tiled=True)  15.5 us
    all_to_all x1, blocking collectives, shards(): rows = lax.all_to_all(copies, near_axes, 0, 0, tiled=True)  10.8 us
    psum x1, blocking collectives, shards(): return lax.psum(partial_out, 'head')  9.14 us
    pallas_call x1, Pallas kernels, shards(): pl.pallas_call(attend_block, out_shape=packed(TOKENS, 2 * HEADS), in_spec...  3.46 us

profile of v3, /device:TPU:1, one launch (start us, length us, event | category | flops | bytes accessed | tf_op | source)
XLA Modules:
  0.0 63.1 jit_solution(6377794072694694737)
XLA Ops:
  0.0 3.5 %attend_block.1 = f32[16,16,128]{2,1,0:T(8,128)S(1)} custom-call(s32[4]{0:T(128)} %lengths.1, s32[4,4]{1,0:T(4,128)} %offsets.1, bf16[4,1,32,128]{3,2,1,0:T(8,128)(2,1)} %bitcast.5, bf16[4,1,128,1024]{3,2,1,0:T(8,128)(2,1)} %keys.1, bf16[4,1,128,1024]{3,2,1,0:T(8,128)(2,1)} %values.1), custom_call_target="tpu_custom_call" | custom-call | tf_op jit(solution)/shard_map/attend_block/pallas_call | solution.py:112
  3.5 15.5 %all_to_all.15.parts = f32[16,16,128]{2,1,0:T(8,128)S(1)} all-to-all(f32[16,16,128]{2,1,0:T(8,128)S(1)} %attend_block.1), channel_id=1, replica_groups=mesh['y'=4,'far'=8,'near'=2,'core'=2,'head'=4] {'y','near','core'}, dimensions={0} | all-to-all | bytes 262144 | tf_op jit(solution)/shard_map/all_to_all | solution.py:130
  19.0 0.2 merge_near.1
  19.1 23.7 %all_to_all.16.parts = f32[8,16,128]{2,1,0:T(8,128)S(1)} all-to-all(f32[8,16,128]{2,1,0:T(8,128)S(1)} %merge_near.1), channel_id=1, replica_groups=mesh['y'=4,'far'=8,'near'=2,'core'=2,'head'=4] {'far'}, dimensions={0} | all-to-all | bytes 131072 | tf_op jit(solution)/shard_map/all_to_all | solution.py:135
  42.8 0.0 copy-start
  42.8 0.2 merge_far.1
  43.0 10.8 %all_to_all.17 = f32[16,8,128]{2,1,0:T(8,128)S(1)} all-to-all(f32[16,8,128]{2,1,0:T(8,128)S(1)} %merge_far.1), channel_id=1, replica_groups=mesh['y'=4,'far'=8,'near'=2,'core'=2,'head'=4] {'y','near','core'}, dimensions={0} | all-to-all | bytes 131072 | tf_op jit(solution)/shard_map/all_to_all | solution.py:140
  53.8 0.0 copy-done
  53.8 0.2 project.1
  53.9 9.1 %psum.7 = f32[4,4,64]{2,1,0:T(4,128)} all-reduce(f32[4,4,64]{2,1,0:T(4,128)S(1)} %project.1), channel_id=1, replica_groups=mesh['y'=4,'far'=8,'near'=2,'core'=2,'head'=4] {'head'}, use_global_device_ids=true, to_apply=%region_0.0 | all-reduce | flops 1024 | bytes 8192 | tf_op jit(solution)/shard_map/psum | solution.py:149
Async XLA Ops:
  42.8 11.0 %copy-start = (bf16[1,8,128,64]{2,3,1,0:T(8,128)(2,1)S(1)}, bf16[1,8,128,64]{2,3,1,0:T(8,128)(2,1)}, u32[]{:S(2)}) copy-start(bf16[1,8,128,64]{2,3,1,0:T(8,128)(2,1)} %param.11) | copy-start | bytes 393220

commit v4 on v3

--- a/solution.py
+++ b/solution.py
@@ -10,6 +10,9 @@
 BATCH, DRAFT, HEADS, ROWS, DH, CTX_DEV, COLS = 4, 4, 8, 32, 128, 1024, 64
 TOKENS = BATCH * DRAFT
 LANES = 128
+near_order = [[11, 0, 1, 2, 3, 4, 5, 6, 7, 8, 9, 10, 12, 13, 14, 15]]
+far_order = [[4, 5, 6, 7, 0, 1, 2, 3]]
+head_order = [[2, 3, 0, 1]]
 near_axes = ("y", "near", "core")
 vmem = pl.BlockSpec(memory_space=pltpu.VMEM)
 hbm = pl.BlockSpec(memory_space=pltpu.HBM)
@@ -102,7 +105,14 @@
         total += lax.dot_general(
             rows, out_proj[0, h], (((1,), (1,)), ((), ())), preferred_element_type=jnp.float32
         )
-    out[...] = total.reshape(BATCH, DRAFT, COLS)
+    packed = jnp.concatenate([total[: TOKENS // 2], total[TOKENS // 2 :]], axis=1)
+    out[...] = jnp.broadcast_to(packed[None], out.shape)
+
+
+def add_groups(terms, out):
+    packed = jnp.sum(terms[...], axis=0)
+    out[: BATCH // 2] = packed[:, :COLS].reshape(BATCH // 2, DRAFT, COLS)
+    out[BATCH // 2 :] = packed[:, COLS:].reshape(BATCH // 2, DRAFT, COLS)
 
 
 def shards(queries, keys, values, lengths, offsets, out_proj):
@@ -127,26 +137,34 @@
         compiler_params=attend_params,
         name="attend_block",
     )(*(in_hbm(x) for x in (lengths, offsets, queries.swapaxes(2, 3), keys, values)))
-    parts = lax.all_to_all(block, near_axes, 0, 0, tiled=True)
+    parts = lax.all_to_all(block, near_axes, 0, 0, axis_index_groups=near_order, tiled=True)
     copies = pl.pallas_call(
         merge_near, out_shape=packed(FAR, 2 * HEADS), in_specs=[vmem], out_specs=vmem,
         compiler_params=small_params, name="merge_near"
     )(parts)
-    parts = lax.all_to_all(copies, "far", 0, 0, tiled=True)
+    parts = lax.all_to_all(copies, "far", 0, 0, axis_index_groups=far_order, tiled=True)
     copies = pl.pallas_call(
         merge_far, out_shape=packed(TOKENS, HEADS), in_specs=[vmem], out_specs=vmem,
         compiler_params=small_params, name="merge_far"
     )(parts)
-    rows = lax.all_to_all(copies, near_axes, 0, 0, tiled=True)
-    partial_out = pl.pallas_call(
+    rows = lax.all_to_all(copies, near_axes, 0, 0, axis_index_groups=near_order, tiled=True)
+    copies = pl.pallas_call(
         project,
-        out_shape=jax.ShapeDtypeStruct((BATCH, DRAFT, COLS), jnp.float32),
+        out_shape=packed(HEAD, TOKENS * COLS // LANES),
         in_specs=[vmem, vmem],
         out_specs=vmem,
         compiler_params=small_params,
         name="project",
     )(rows.reshape(TOKENS * HEADS, LANES), out_proj.swapaxes(2, 3))
-    return lax.psum(partial_out, "head")
+    terms = lax.all_to_all(copies, "head", 0, 0, axis_index_groups=head_order, tiled=True)
+    return pl.pallas_call(
+        add_groups,
+        out_shape=jax.ShapeDtypeStruct((BATCH, DRAFT, COLS), jnp.float32),
+        in_specs=[vmem],
+        out_specs=vmem,
+        compiler_params=small_params,
+        name="add_groups",
+    )(terms)
 
 
 def solution(mesh):

time: 63.3 us -> 52.3 us (0.83)
  blocking collectives: 59.1 us -> 47.4 us
  Pallas kernels: 3.94 us -> 4.68 us
    psum x1 -> x0, blocking collectives: 9.14 us -> none  [shards(): return lax.psum(partial_out, 'head')]
    all_to_all x3 -> x4, blocking collectives: 50 us -> 47.4 us  [the longest x1 15.8 us: shards(): lax.all_to_all(copies, 'far', 0, 0, axis_index_groups=far_order, tiled=True)]
    pallas_call x1 -> x2, Pallas kernels: 0.17 us -> 0.91 us  [the longest x1 0.67 us: shards(): pl.pallas_call(add_groups, out_shape=jax.ShapeDtypeStruct((BATCH, DRAFT,...]
where the time goes in v4:
time: 52.3 us; the launch traced here: 52.1 us
  blocking collectives  47.4 us (91%)
  Pallas kernels  4.68 us (9%)
    all_to_all x1, blocking collectives, shards(): lax.all_to_all(copies, 'far', 0, 0, axis_index_groups=far_order, tiled=True)  15.8 us
    all_to_all x1, blocking collectives, shards(): lax.all_to_all(block, near_axes, 0, 0, axis_index_groups=near_order, tile...  14.8 us
    all_to_all x1, blocking collectives, shards(): lax.all_to_all(copies, near_axes, 0, 0, axis_index_groups=near_order, til...  9.92 us
    all_to_all x1, blocking collectives, shards(): lax.all_to_all(copies, 'head', 0, 0, axis_index_groups=head_order, tiled=...  6.87 us
    pallas_call x1, Pallas kernels, shards(): pl.pallas_call(attend_block, out_shape=packed(TOKENS, 2 * HEADS), in_spec...  3.46 us

profile of v4, /device:TPU:1, one launch (start us, length us, event | category | flops | bytes accessed | tf_op | source)
XLA Modules:
  0.0 52.1 jit_solution(14057908482675195880)
XLA Ops:
  0.0 3.5 %attend_block.1 = f32[16,16,128]{2,1,0:T(8,128)S(1)} custom-call(s32[4]{0:T(128)} %lengths.1, s32[4,4]{1,0:T(4,128)} %offsets.1, bf16[4,1,32,128]{3,2,1,0:T(8,128)(2,1)} %bitcast.5, bf16[4,1,128,1024]{3,2,1,0:T(8,128)(2,1)} %keys.1, bf16[4,1,128,1024]{3,2,1,0:T(8,128)(2,1)} %values.1), custom_call_target="tpu_custom_call" | custom-call | tf_op jit(solution)/shard_map/attend_block/pallas_call | solution.py:122
  3.5 14.8 %all_to_all.20.parts = f32[16,16,128]{2,1,0:T(8,128)S(1)} all-to-all(f32[16,16,128]{2,1,0:T(8,128)S(1)} %attend_block.1), channel_id=1, replica_groups={{268,0,4,8,12,128,132,136,140,256,260,264,384,388,392,396},{269,1,5,9,1..., dimensions={0} | all-to-all | bytes 262144 | tf_op jit(solution)/shard_map/all_to_all | solution.py:140
  18.3 0.2 merge_near.1
  18.4 15.8 %all_to_all.21.parts = f32[8,16,128]{2,1,0:T(8,128)S(1)} all-to-all(f32[8,16,128]{2,1,0:T(8,128)S(1)} %merge_near.1), channel_id=1, replica_groups={{64,80,96,112,0,16,32,48},{65,81,97,113,1,17,33,49},{66,82,98,114,2,18,..., dimensions={0} | all-to-all | bytes 131072 | tf_op jit(solution)/shard_map/all_to_all | solution.py:145
  34.2 0.0 copy-start
  34.2 0.2 merge_far.1
  34.4 9.9 %all_to_all.22 = f32[16,8,128]{2,1,0:T(8,128)S(1)} all-to-all(f32[16,8,128]{2,1,0:T(8,128)S(1)} %merge_far.1), channel_id=1, replica_groups={{268,0,4,8,12,128,132,136,140,256,260,264,384,388,392,396},{269,1,5,9,1..., dimensions={0} | all-to-all | bytes 131072 | tf_op jit(solution)/shard_map/all_to_all | solution.py:150
  44.3 0.0 copy-done
  44.3 0.2 project.1
  44.5 6.9 %all_to_all.23.terms = f32[4,8,128]{2,1,0:T(8,128)S(1)} all-to-all(f32[4,8,128]{2,1,0:T(8,128)S(1)} %project.1), channel_id=1, replica_groups={{2,3,0,1},{6,7,4,5},{10,11,8,9},{14,15,12,13},{18,19,16,17},{22,23,20,2..., dimensions={0} | all-to-all | bytes 32768 | tf_op jit(solution)/shard_map/all_to_all | solution.py:159
  51.4 0.7 %add_groups.1 = f32[4,4,64]{2,1,0:T(4,128)} custom-call(f32[4,8,128]{2,1,0:T(8,128)S(1)} %all_to_all.23.terms), custom_call_target="tpu_custom_call" | custom-call | tf_op jit(solution)/shard_map/add_groups/pallas_call | solution.py:160
Async XLA Ops:
  34.2 10.1 %copy-start = (bf16[1,8,128,64]{2,3,1,0:T(8,128)(2,1)S(1)}, bf16[1,8,128,64]{2,3,1,0:T(8,128)(2,1)}, u32[]{:S(2)}) copy-start(bf16[1,8,128,64]{2,3,1,0:T(8,128)(2,1)} %param.11) | copy-start | bytes 393220

commit v5 on v4

--- a/solution.py
+++ b/solution.py
@@ -10,8 +10,12 @@
 BATCH, DRAFT, HEADS, ROWS, DH, CTX_DEV, COLS = 4, 4, 8, 32, 128, 1024, 64
 TOKENS = BATCH * DRAFT
 LANES = 128
-near_order = [[11, 0, 1, 2, 3, 4, 5, 6, 7, 8, 9, 10, 12, 13, 14, 15]]
-far_order = [[4, 5, 6, 7, 0, 1, 2, 3]]
+SLOT = LANES // HEADS
+MESSAGE = (HEADS + 1) * LANES
+spread_order = [11, 0, 1, 2, 3, 4, 5, 6, 7, 8, 9, 10, 12, 13, 14, 15]
+far_order = [9, 11, 13, 15, 1, 3, 5, 7, 8, 10, 12, 14, 0, 2, 4, 6]
+far_halves = (1, 0)
+gather_order = [5, 0, 1, 2, 3, 4, 6, 7]
 head_order = [[2, 3, 0, 1]]
 near_axes = ("y", "near", "core")
 vmem = pl.BlockSpec(memory_space=pltpu.VMEM)
@@ -24,18 +28,21 @@
     return pltpu.with_memory_space_constraint(x, pltpu.HBM)
 
 
-def pack_stats(top, total):
-    lane = lax.broadcasted_iota(jnp.int32, top.shape[:-1] + (LANES,), top.ndim - 1)
-    return jnp.where(lane < LANES // 2, top, total)
-
-
-def merge(parts):
-    stats = parts[:, HEADS:, :]
-    tops = stats[:, :, :1]
-    top = jnp.max(tops, axis=0)
-    factor = jnp.exp(tops - top[None])
-    total = jnp.sum(factor * stats[:, :, LANES // 2 : LANES // 2 + 1], axis=0)
-    summed = jnp.sum(factor * parts[:, :HEADS, :], axis=0)
+def stat_lanes(count):
+    lane = lax.broadcasted_iota(jnp.int32, (count, LANES), 1)
+    return lane // SLOT, lax.rem(lane, SLOT) < SLOT // 2
+
+
+def merge(parts, some):
+    stats = parts[some, 0, HEADS * LANES :]
+    top = jnp.max(stats, axis=0, keepdims=True)
+    factor = jnp.exp(stats - top)
+    sums = pltpu.roll(stats, LANES - SLOT // 2, 1)
+    total = jnp.sum(factor * sums, axis=0, keepdims=True)
+    summed = []
+    for h in range(HEADS):
+        terms = factor[:, h * SLOT : h * SLOT + 1] * parts[some, 0, h * LANES : (h + 1) * LANES]
+        summed.append(jnp.sum(terms, axis=0, keepdims=True))
     return top, total, summed
 
 
@@ -60,11 +67,14 @@
     index = chip * CORES + lax.axis_index("core")
     positions = index * CTX_DEV + lax.broadcasted_iota(jnp.int32, (ROWS, CTX_DEV), 1)
     draft = lax.broadcasted_iota(jnp.int32, (ROWS, 1), 0) // HEADS
+    head = lax.rem(lax.broadcasted_iota(jnp.int32, (ROWS, LANES), 0), HEADS)
+    slot, is_top = stat_lanes(ROWS)
     for copy in small:
+        copy.wait()
+    for copy in key_copies:
         copy.wait()
     weights = []
     for b in range(BATCH):
-        key_copies[b].wait()
         scores = jnp.dot(held_queries[b, 0], held_keys[b], preferred_element_type=jnp.float32)
         scores = scores * DH ** (-0.5)
         offset = jnp.full((ROWS, 1), held_offsets[b, 0], jnp.int32)
@@ -76,26 +86,40 @@
         weight = jnp.where(seen, jnp.exp(scores - block_max), 0.0)
         block_sum = jnp.sum(weight, axis=1, keepdims=True)
         weights.append(weight.astype(jnp.bfloat16))
-        out[pl.ds(b * DRAFT, DRAFT), HEADS:, :] = pack_stats(block_max, block_sum).reshape(
-            DRAFT, HEADS, LANES
-        )
+        stats = jnp.where(is_top, block_max, block_sum)
+        stats = jnp.where(head == slot, stats, 0.0).reshape(DRAFT, HEADS, LANES)
+        stats = jnp.sum(stats, axis=1)
+        for j in range(DRAFT):
+            out[b * DRAFT + j, :, HEADS * LANES :] = stats[j : j + 1]
+    for copy in value_copies:
+        copy.wait()
     for b in range(BATCH):
-        value_copies[b].wait()
         block_out = lax.dot_general(
             weights[b], held_values[b], (((1,), (1,)), ((), ())), preferred_element_type=jnp.float32
         )
-        out[pl.ds(b * DRAFT, DRAFT), :HEADS, :] = block_out.reshape(DRAFT, HEADS, LANES)
+        for j in range(DRAFT):
+            for h in range(HEADS):
+                row = block_out[j * HEADS + h : j * HEADS + h + 1]
+                out[b * DRAFT + j, :, h * LANES : (h + 1) * LANES] = row
 
 
 def merge_near(parts, out):
-    top, total, summed = merge(parts)
-    out[:, :HEADS, :] = jnp.broadcast_to(summed[None], (FAR, HEADS, LANES))
-    out[:, HEADS:, :] = jnp.broadcast_to(pack_stats(top, total)[None], (FAR, HEADS, LANES))
+    top, total, summed = merge(parts, slice(0, TOKENS))
+    _, is_top = stat_lanes(1)
+    stats = jnp.where(is_top, top, pltpu.roll(total, SLOT // 2, 1))
+    for h, row in enumerate(summed + [stats]):
+        for i in range(FAR * NEAR):
+            out[i, :, h * LANES : (h + 1) * LANES] = row
 
 
 def merge_far(parts, out):
-    _, total, summed = merge(parts)
-    out[...] = jnp.broadcast_to((summed / total)[None], out.shape)
+    for q in range(NEAR):
+        _, total, summed = merge(parts, slice(q * FAR, (q + 1) * FAR))
+        rows = [row / total[:, h * SLOT : h * SLOT + 1] for h, row in enumerate(summed)]
+        rows = jnp.concatenate(rows, axis=0)
+        out[:, q * HEADS : (q + 1) * HEADS, :] = jnp.broadcast_to(
+            rows[None], (Y * CORES, HEADS, LANES)
+        )
 
 
 def project(attended, out_proj, out):
@@ -105,7 +129,12 @@
         total += lax.dot_general(
             rows, out_proj[0, h], (((1,), (1,)), ((), ())), preferred_element_type=jnp.float32
         )
-    packed = jnp.concatenate([total[: TOKENS // 2], total[TOKENS // 2 :]], axis=1)
+    came = [(pair // CORES, q, pair % CORES) for pair in gather_order for q in far_halves]
+    at = [came.index((d // (NEAR * CORES), d // CORES % NEAR, d % CORES)) for d in spread_order]
+    rows = [total[i : i + 1] for i in at]
+    packed = jnp.concatenate(
+        [jnp.concatenate(half, axis=0) for half in (rows[: TOKENS // 2], rows[TOKENS // 2 :])], axis=1
+    )
     out[...] = jnp.broadcast_to(packed[None], out.shape)
 
 
@@ -116,12 +145,12 @@
 
 
 def shards(queries, keys, values, lengths, offsets, out_proj):
-    def packed(copies, rows):
-        return jax.ShapeDtypeStruct((copies, rows, LANES), jnp.float32)
+    def packed(*shape):
+        return jax.ShapeDtypeStruct(shape, jnp.float32)
 
     block = pl.pallas_call(
         attend_block,
-        out_shape=packed(TOKENS, 2 * HEADS),
+        out_shape=packed(TOKENS, 1, MESSAGE),
         in_specs=[hbm] * 5,
         out_specs=vmem,
         scratch_shapes=[
@@ -137,20 +166,20 @@
         compiler_params=attend_params,
         name="attend_block",
     )(*(in_hbm(x) for x in (lengths, offsets, queries.swapaxes(2, 3), keys, values)))
-    parts = lax.all_to_all(block, near_axes, 0, 0, axis_index_groups=near_order, tiled=True)
+    parts = lax.all_to_all(block, near_axes, 0, 0, axis_index_groups=[spread_order], tiled=True)
     copies = pl.pallas_call(
-        merge_near, out_shape=packed(FAR, 2 * HEADS), in_specs=[vmem], out_specs=vmem,
+        merge_near, out_shape=packed(FAR * NEAR, 1, MESSAGE), in_specs=[vmem], out_specs=vmem,
         compiler_params=small_params, name="merge_near"
     )(parts)
-    parts = lax.all_to_all(copies, "far", 0, 0, axis_index_groups=far_order, tiled=True)
+    parts = lax.all_to_all(copies, ("far", "near"), 0, 0, axis_index_groups=[far_order], tiled=True)
     copies = pl.pallas_call(
-        merge_far, out_shape=packed(TOKENS, HEADS), in_specs=[vmem], out_specs=vmem,
+        merge_far, out_shape=packed(Y * CORES, NEAR * HEADS, LANES), in_specs=[vmem], out_specs=vmem,
         compiler_params=small_params, name="merge_far"
     )(parts)
-    rows = lax.all_to_all(copies, near_axes, 0, 0, axis_index_groups=near_order, tiled=True)
+    rows = lax.all_to_all(copies, ("y", "core"), 0, 0, axis_index_groups=[gather_order], tiled=True)
     copies = pl.pallas_call(
         project,
-        out_shape=packed(HEAD, TOKENS * COLS // LANES),
+        out_shape=packed(HEAD, TOKENS * COLS // LANES, LANES),
         in_specs=[vmem, vmem],
         out_specs=vmem,
         compiler_params=small_params,

time: 52.3 us -> 51.1 us (0.977)
  Pallas kernels: 4.68 us -> 3.74 us
    pallas_call x4, Pallas kernels: 4.01 us -> 3.07 us  [the longest x1 2.49 us: shards(): pl.pallas_call(attend_block, out_shape=packed(TOKENS, 1, MESSAGE), in_spe...]
where the time goes in v5:
time: 51.1 us; the launch traced here: 50.7 us
  blocking collectives  46.9 us (92%)
  Pallas kernels  3.74 us (7%)
    all_to_all x1, blocking collectives, shards(): lax.all_to_all(copies, ('far', 'near'), 0, 0, axis_index_groups=[far_orde...  17.5 us
    all_to_all x1, blocking collectives, shards(): lax.all_to_all(block, near_axes, 0, 0, axis_index_groups=[spread_order],...  14.4 us
    all_to_all x1, blocking collectives, shards(): lax.all_to_all(copies, ('y', 'core'), 0, 0, axis_index_groups=[gather_ord...  8.53 us
    all_to_all x1, blocking collectives, shards(): lax.all_to_all(copies, 'head', 0, 0, axis_index_groups=head_order, tiled=...  6.57 us
    pallas_call x1, Pallas kernels, shards(): pl.pallas_call(attend_block, out_shape=packed(TOKENS, 1, MESSAGE), in_spe...  2.49 us

profile of v5, /device:TPU:1, one launch (start us, length us, event | category | flops | bytes accessed | tf_op | source)
XLA Modules:
  0.0 50.7 jit_solution(18049604317184360655)
XLA Ops:
  0.0 2.5 %attend_block.1 = f32[16,1,1152]{2,1,0:T(1,128)S(1)} custom-call(s32[4]{0:T(128)} %lengths.1, s32[4,4]{1,0:T(4,128)} %offsets.1, bf16[4,1,32,128]{3,2,1,0:T(8,128)(2,1)} %bitcast.5, bf16[4,1,128,1024]{3,2,1,0:T(8,128)(2,1)} %keys.1, bf16[4,1,128,1024]{3,2,1,0:T(8,128)(2,1)} %values.1), custom_call_target="tpu_custom_call" | custom-call | tf_op jit(solution)/shard_map/attend_block/pallas_call | solution.py:151
  2.5 14.4 %all_to_all.20.parts = f32[16,1,1152]{2,1,0:T(1,128)S(1)} all-to-all(f32[16,1,1152]{2,1,0:T(1,128)S(1)} %attend_block.1), channel_id=1, replica_groups={{268,0,4,8,12,128,132,136,140,256,260,264,384,388,392,396},{269,1,5,9,1..., dimensions={0} | all-to-all | bytes 147456 | tf_op jit(solution)/shard_map/all_to_all | solution.py:169
  16.9 0.2 merge_near.1
  17.0 17.5 %all_to_all.21.parts = f32[16,1,1152]{2,1,0:T(1,128)S(1)} all-to-all(f32[16,1,1152]{2,1,0:T(1,128)S(1)} %merge_near.1), channel_id=1, replica_groups={{72,88,104,120,8,24,40,56,64,80,96,112,0,16,32,48},{73,89,105,121,9,25,..., dimensions={0} | all-to-all | bytes 147456 | tf_op jit(solution)/shard_map/all_to_all | solution.py:174
  34.5 0.0 copy-start
  34.5 0.2 merge_far.1
  34.7 8.5 %all_to_all.22 = f32[8,16,128]{2,1,0:T(8,128)S(1)} all-to-all(f32[8,16,128]{2,1,0:T(8,128)S(1)} %merge_far.1), channel_id=1, replica_groups={{260,0,4,128,132,256,384,388},{261,1,5,129,133,257,385,389},{262,2,6,13..., dimensions={0} | all-to-all | bytes 131072 | tf_op jit(solution)/shard_map/all_to_all | solution.py:179
  43.2 0.0 copy-done
  43.2 0.2 project.1
  43.4 6.6 %all_to_all.23.terms = f32[4,8,128]{2,1,0:T(8,128)S(1)} all-to-all(f32[4,8,128]{2,1,0:T(8,128)S(1)} %project.1), channel_id=1, replica_groups={{2,3,0,1},{6,7,4,5},{10,11,8,9},{14,15,12,13},{18,19,16,17},{22,23,20,2..., dimensions={0} | all-to-all | bytes 32768 | tf_op jit(solution)/shard_map/all_to_all | solution.py:188
  50.0 0.7 %add_groups.1 = f32[4,4,64]{2,1,0:T(4,128)} custom-call(f32[4,8,128]{2,1,0:T(8,128)S(1)} %all_to_all.23.terms), custom_call_target="tpu_custom_call" | custom-call | tf_op jit(solution)/shard_map/add_groups/pallas_call | solution.py:189
Async XLA Ops:
  34.5 8.7 %copy-start = (bf16[1,8,128,64]{2,3,1,0:T(8,128)(2,1)S(1)}, bf16[1,8,128,64]{2,3,1,0:T(8,128)(2,1)}, u32[]{:S(2)}) copy-start(bf16[1,8,128,64]{2,3,1,0:T(8,128)(2,1)} %param.11) | copy-start | bytes 393220

commit v6 on v5

--- a/solution.py
+++ b/solution.py
@@ -6,6 +6,7 @@
 from jax.sharding import Mesh, PartitionSpec as P
 
 masked_score = -1e30
+left_out = -3e38
 Y, FAR, NEAR, CORES, HEAD = 4, 8, 2, 2, 4
 BATCH, DRAFT, HEADS, ROWS, DH, CTX_DEV, COLS = 4, 4, 8, 32, 128, 1024, 64
 TOKENS = BATCH * DRAFT
@@ -13,8 +14,8 @@
 SLOT = LANES // HEADS
 MESSAGE = (HEADS + 1) * LANES
 spread_order = [11, 0, 1, 2, 3, 4, 5, 6, 7, 8, 9, 10, 12, 13, 14, 15]
-far_order = [9, 11, 13, 15, 1, 3, 5, 7, 8, 10, 12, 14, 0, 2, 4, 6]
-far_halves = (1, 0)
+far_order = [9, 8, 11, 10, 13, 12, 15, 14, 1, 0, 3, 2, 5, 4, 7, 6]
+far_turns = (1, 0)
 gather_order = [5, 0, 1, 2, 3, 4, 6, 7]
 head_order = [[2, 3, 0, 1]]
 near_axes = ("y", "near", "core")
@@ -33,35 +34,31 @@
     return lane // SLOT, lax.rem(lane, SLOT) < SLOT // 2
 
 
-def merge(parts, some):
-    stats = parts[some, 0, HEADS * LANES :]
-    top = jnp.max(stats, axis=0, keepdims=True)
-    factor = jnp.exp(stats - top)
+def merge(parts, some=None):
+    stats = parts[:, 0, HEADS * LANES :]
+    counted = stats if some is None else jnp.where(some, stats, left_out)
+    top = jnp.max(counted, axis=0, keepdims=True)
+    factor = jnp.exp(counted - top)
     sums = pltpu.roll(stats, LANES - SLOT // 2, 1)
     total = jnp.sum(factor * sums, axis=0, keepdims=True)
     summed = []
     for h in range(HEADS):
-        terms = factor[:, h * SLOT : h * SLOT + 1] * parts[some, 0, h * LANES : (h + 1) * LANES]
+        terms = factor[:, h * SLOT : h * SLOT + 1] * parts[:, 0, h * LANES : (h + 1) * LANES]
         summed.append(jnp.sum(terms, axis=0, keepdims=True))
     return top, total, summed
 
 
 def attend_block(lengths, offsets, queries, keys, values, out, *scratch):
-    held_lengths, held_offsets, held_queries, held_keys, held_values, small_sems, key_sems, value_sems = scratch
+    held_lengths, held_offsets, held_queries, held_keys, held_values, small_sems, key_sem, value_sem = scratch
     small = [
         pltpu.make_async_copy(source, target, small_sems.at[i])
         for i, (source, target) in enumerate(
             ((queries, held_queries), (lengths, held_lengths), (offsets, held_offsets))
         )
     ]
-    key_copies = [
-        pltpu.make_async_copy(keys.at[b, 0], held_keys.at[b], key_sems.at[b]) for b in range(BATCH)
-    ]
-    value_copies = [
-        pltpu.make_async_copy(values.at[b, 0], held_values.at[b], value_sems.at[b])
-        for b in range(BATCH)
-    ]
-    for copy in small + key_copies + value_copies:
+    key_copy = pltpu.make_async_copy(keys, held_keys, key_sem)
+    value_copy = pltpu.make_async_copy(values, held_values, value_sem)
+    for copy in small + [key_copy, value_copy]:
         copy.start()
     chip = (lax.axis_index("y") * FAR + lax.axis_index("far")) * NEAR + lax.axis_index("near")
     index = chip * CORES + lax.axis_index("core")
@@ -71,11 +68,10 @@
     slot, is_top = stat_lanes(ROWS)
     for copy in small:
         copy.wait()
-    for copy in key_copies:
-        copy.wait()
+    key_copy.wait()
     weights = []
     for b in range(BATCH):
-        scores = jnp.dot(held_queries[b, 0], held_keys[b], preferred_element_type=jnp.float32)
+        scores = jnp.dot(held_queries[b, 0], held_keys[b, 0], preferred_element_type=jnp.float32)
         scores = scores * DH ** (-0.5)
         offset = jnp.full((ROWS, 1), held_offsets[b, 0], jnp.int32)
         for j in range(1, DRAFT):
@@ -91,11 +87,11 @@
         stats = jnp.sum(stats, axis=1)
         for j in range(DRAFT):
             out[b * DRAFT + j, :, HEADS * LANES :] = stats[j : j + 1]
-    for copy in value_copies:
-        copy.wait()
+    value_copy.wait()
     for b in range(BATCH):
         block_out = lax.dot_general(
-            weights[b], held_values[b], (((1,), (1,)), ((), ())), preferred_element_type=jnp.float32
+            weights[b],
+            held_values[b, 0], (((1,), (1,)), ((), ())), preferred_element_type=jnp.float32
         )
         for j in range(DRAFT):
             for h in range(HEADS):
@@ -104,7 +100,7 @@
 
 
 def merge_near(parts, out):
-    top, total, summed = merge(parts, slice(0, TOKENS))
+    top, total, summed = merge(parts)
     _, is_top = stat_lanes(1)
     stats = jnp.where(is_top, top, pltpu.roll(total, SLOT // 2, 1))
     for h, row in enumerate(summed + [stats]):
@@ -113,8 +109,9 @@
 
 
 def merge_far(parts, out):
+    source = lax.broadcasted_iota(jnp.int32, (FAR * NEAR, LANES), 0)
     for q in range(NEAR):
-        _, total, summed = merge(parts, slice(q * FAR, (q + 1) * FAR))
+        _, total, summed = merge(parts, lax.rem(source, NEAR) == q)
         rows = [row / total[:, h * SLOT : h * SLOT + 1] for h, row in enumerate(summed)]
         rows = jnp.concatenate(rows, axis=0)
         out[:, q * HEADS : (q + 1) * HEADS, :] = jnp.broadcast_to(
@@ -129,7 +126,7 @@
         total += lax.dot_general(
             rows, out_proj[0, h], (((1,), (1,)), ((), ())), preferred_element_type=jnp.float32
         )
-    came = [(pair // CORES, q, pair % CORES) for pair in gather_order for q in far_halves]
+    came = [(pair // CORES, q, pair % CORES) for pair in gather_order for q in far_turns]
     at = [came.index((d // (NEAR * CORES), d // CORES % NEAR, d % CORES)) for d in spread_order]
     rows = [total[i : i + 1] for i in at]
     packed = jnp.concatenate(
@@ -157,11 +154,11 @@
             pltpu.SMEM((BATCH,), jnp.int32),
             pltpu.SMEM((BATCH, DRAFT), jnp.int32),
             pltpu.VMEM((BATCH, 1, ROWS, DH), jnp.bfloat16),
-            pltpu.VMEM((BATCH, DH, CTX_DEV), jnp.bfloat16),
-            pltpu.VMEM((BATCH, DH, CTX_DEV), jnp.bfloat16),
+            pltpu.VMEM((BATCH, 1, DH, CTX_DEV), jnp.bfloat16),
+            pltpu.VMEM((BATCH, 1, DH, CTX_DEV), jnp.bfloat16),
             pltpu.SemaphoreType.DMA((3,)),
-            pltpu.SemaphoreType.DMA((BATCH,)),
-            pltpu.SemaphoreType.DMA((BATCH,)),
+            pltpu.SemaphoreType.DMA,
+            pltpu.SemaphoreType.DMA,
         ],
         compiler_params=attend_params,
         name="attend_block",

time: 51.1 us -> 50.9 us (level)
    all_to_all x1, blocking collectives: 8.53 us -> 7.8 us  [shards(): lax.all_to_all(copies, ('y', 'core'), 0, 0, axis_index_groups=[gather_ord...]
    all_to_all x1, blocking collectives: 17.5 us -> 18 us  [shards(): lax.all_to_all(copies, ('far', 'near'), 0, 0, axis_index_groups=[far_orde...]
where the time goes in v6:
time: 50.9 us; the launch traced here: 50.3 us
  blocking collectives  46.8 us (92%)
  Pallas kernels  3.49 us (7%)
    all_to_all x1, blocking collectives, shards(): lax.all_to_all(copies, ('far', 'near'), 0, 0, axis_index_groups=[far_orde...  18 us
    all_to_all x1, blocking collectives, shards(): lax.all_to_all(block, near_axes, 0, 0, axis_index_groups=[spread_order],...  14.4 us
    all_to_all x1, blocking collectives, shards(): lax.all_to_all(copies, ('y', 'core'), 0, 0, axis_index_groups=[gather_ord...  7.8 us
    all_to_all x1, blocking collectives, shards(): lax.all_to_all(copies, 'head', 0, 0, axis_index_groups=head_order, tiled=...  6.57 us
    pallas_call x1, Pallas kernels, shards(): pl.pallas_call(attend_block, out_shape=packed(TOKENS, 1, MESSAGE), in_spe...  2.24 us

profile of v6, /device:TPU:1, one launch (start us, length us, event | category | flops | bytes accessed | tf_op | source)
XLA Modules:
  0.0 50.3 jit_solution(14519326986812565358)
XLA Ops:
  0.0 2.2 %attend_block.1 = f32[16,1,1152]{2,1,0:T(1,128)S(1)} custom-call(s32[4]{0:T(128)} %lengths.1, s32[4,4]{1,0:T(4,128)} %offsets.1, bf16[4,1,32,128]{3,2,1,0:T(8,128)(2,1)} %bitcast.5, bf16[4,1,128,1024]{3,2,1,0:T(8,128)(2,1)} %keys.1, bf16[4,1,128,1024]{3,2,1,0:T(8,128)(2,1)} %values.1), custom_call_target="tpu_custom_call" | custom-call | tf_op jit(solution)/shard_map/attend_block/pallas_call | solution.py:148
  2.2 14.4 %all_to_all.20.parts = f32[16,1,1152]{2,1,0:T(1,128)S(1)} all-to-all(f32[16,1,1152]{2,1,0:T(1,128)S(1)} %attend_block.1), channel_id=1, replica_groups={{268,0,4,8,12,128,132,136,140,256,260,264,384,388,392,396},{269,1,5,9,1..., dimensions={0} | all-to-all | bytes 147456 | tf_op jit(solution)/shard_map/all_to_all | solution.py:166
  16.6 0.2 merge_near.1
  16.8 18.0 %all_to_all.21.parts = f32[16,1,1152]{2,1,0:T(1,128)S(1)} all-to-all(f32[16,1,1152]{2,1,0:T(1,128)S(1)} %merge_near.1), channel_id=1, replica_groups={{72,64,88,80,104,96,120,112,8,0,24,16,40,32,56,48},{73,65,89,81,105,97,..., dimensions={0} | all-to-all | bytes 147456 | tf_op jit(solution)/shard_map/all_to_all | solution.py:171
  34.8 0.0 copy-start
  34.8 0.2 merge_far.1
  35.0 7.8 %all_to_all.22 = f32[8,16,128]{2,1,0:T(8,128)S(1)} all-to-all(f32[8,16,128]{2,1,0:T(8,128)S(1)} %merge_far.1), channel_id=1, replica_groups={{260,0,4,128,132,256,384,388},{261,1,5,129,133,257,385,389},{262,2,6,13..., dimensions={0} | all-to-all | bytes 131072 | tf_op jit(solution)/shard_map/all_to_all | solution.py:176
  42.8 0.0 copy-done
  42.8 0.2 project.1
  43.0 6.6 %all_to_all.23.terms = f32[4,8,128]{2,1,0:T(8,128)S(1)} all-to-all(f32[4,8,128]{2,1,0:T(8,128)S(1)} %project.1), channel_id=1, replica_groups={{2,3,0,1},{6,7,4,5},{10,11,8,9},{14,15,12,13},{18,19,16,17},{22,23,20,2..., dimensions={0} | all-to-all | bytes 32768 | tf_op jit(solution)/shard_map/all_to_all | solution.py:185
  49.6 0.7 %add_groups.1 = f32[4,4,64]{2,1,0:T(4,128)} custom-call(f32[4,8,128]{2,1,0:T(8,128)S(1)} %all_to_all.23.terms), custom_call_target="tpu_custom_call" | custom-call | tf_op jit(solution)/shard_map/add_groups/pallas_call | solution.py:186
Async XLA Ops:
  34.8 8.0 %copy-start = (bf16[1,8,128,64]{2,3,1,0:T(8,128)(2,1)S(1)}, bf16[1,8,128,64]{2,3,1,0:T(8,128)(2,1)}, u32[]{:S(2)}) copy-start(bf16[1,8,128,64]{2,3,1,0:T(8,128)(2,1)} %param.11) | copy-start | bytes 393220

commit v7 on v6

--- a/solution.py
+++ b/solution.py
@@ -6,17 +6,14 @@
 from jax.sharding import Mesh, PartitionSpec as P
 
 masked_score = -1e30
-left_out = -3e38
 Y, FAR, NEAR, CORES, HEAD = 4, 8, 2, 2, 4
 BATCH, DRAFT, HEADS, ROWS, DH, CTX_DEV, COLS = 4, 4, 8, 32, 128, 1024, 64
 TOKENS = BATCH * DRAFT
 LANES = 128
 SLOT = LANES // HEADS
 MESSAGE = (HEADS + 1) * LANES
-spread_order = [11, 0, 1, 2, 3, 4, 5, 6, 7, 8, 9, 10, 12, 13, 14, 15]
-far_order = [9, 8, 11, 10, 13, 12, 15, 14, 1, 0, 3, 2, 5, 4, 7, 6]
-far_turns = (1, 0)
-gather_order = [5, 0, 1, 2, 3, 4, 6, 7]
+near_order = [[11, 0, 1, 2, 3, 4, 5, 6, 7, 8, 9, 10, 12, 13, 14, 15]]
+far_order = [[5, 6, 7, 0, 1, 2, 3, 4]]
 head_order = [[2, 3, 0, 1]]
 near_axes = ("y", "near", "core")
 vmem = pl.BlockSpec(memory_space=pltpu.VMEM)
@@ -34,11 +31,10 @@
     return lane // SLOT, lax.rem(lane, SLOT) < SLOT // 2
 
 
-def merge(parts, some=None):
+def merge(parts):
     stats = parts[:, 0, HEADS * LANES :]
-    counted = stats if some is None else jnp.where(some, stats, left_out)
-    top = jnp.max(counted, axis=0, keepdims=True)
-    factor = jnp.exp(counted - top)
+    top = jnp.max(stats, axis=0, keepdims=True)
+    factor = jnp.exp(stats - top)
     sums = pltpu.roll(stats, LANES - SLOT // 2, 1)
     total = jnp.sum(factor * sums, axis=0, keepdims=True)
     summed = []
@@ -104,19 +100,14 @@
     _, is_top = stat_lanes(1)
     stats = jnp.where(is_top, top, pltpu.roll(total, SLOT // 2, 1))
     for h, row in enumerate(summed + [stats]):
-        for i in range(FAR * NEAR):
+        for i in range(FAR):
             out[i, :, h * LANES : (h + 1) * LANES] = row
 
 
 def merge_far(parts, out):
-    source = lax.broadcasted_iota(jnp.int32, (FAR * NEAR, LANES), 0)
-    for q in range(NEAR):
-        _, total, summed = merge(parts, lax.rem(source, NEAR) == q)
-        rows = [row / total[:, h * SLOT : h * SLOT + 1] for h, row in enumerate(summed)]
-        rows = jnp.concatenate(rows, axis=0)
-        out[:, q * HEADS : (q + 1) * HEADS, :] = jnp.broadcast_to(
-            rows[None], (Y * CORES, HEADS, LANES)
-        )
+    _, total, summed = merge(parts)
+    rows = [row / total[:, h * SLOT : h * SLOT + 1] for h, row in enumerate(summed)]
+    out[...] = jnp.broadcast_to(jnp.concatenate(rows, axis=0)[None], out.shape)
 
 
 def project(attended, out_proj, out):
@@ -126,12 +117,7 @@
         total += lax.dot_general(
             rows, out_proj[0, h], (((1,), (1,)), ((), ())), preferred_element_type=jnp.float32
         )
-    came = [(pair // CORES, q, pair % CORES) for pair in gather_order for q in far_turns]
-    at = [came.index((d // (NEAR * CORES), d // CORES % NEAR, d % CORES)) for d in spread_order]
-    rows = [total[i : i + 1] for i in at]
-    packed = jnp.concatenate(
-        [jnp.concatenate(half, axis=0) for half in (rows[: TOKENS // 2], rows[TOKENS // 2 :])], axis=1
-    )
+    packed = jnp.concatenate([total[: TOKENS // 2], total[TOKENS // 2 :]], axis=1)
     out[...] = jnp.broadcast_to(packed[None], out.shape)
 
 
@@ -163,17 +149,17 @@
         compiler_params=attend_params,
         name="attend_block",
     )(*(in_hbm(x) for x in (lengths, offsets, queries.swapaxes(2, 3), keys, values)))
-    parts = lax.all_to_all(block, near_axes, 0, 0, axis_index_groups=[spread_order], tiled=True)
+    parts = lax.all_to_all(block, near_axes, 0, 0, axis_index_groups=near_order, tiled=True)
     copies = pl.pallas_call(
-        merge_near, out_shape=packed(FAR * NEAR, 1, MESSAGE), in_specs=[vmem], out_specs=vmem,
+        merge_near, out_shape=packed(FAR, 1, MESSAGE), in_specs=[vmem], out_specs=vmem,
         compiler_params=small_params, name="merge_near"
     )(parts)
-    parts = lax.all_to_all(copies, ("far", "near"), 0, 0, axis_index_groups=[far_order], tiled=True)
+    parts = lax.all_to_all(copies, "far", 0, 0, axis_index_groups=far_order, tiled=True)
     copies = pl.pallas_call(
-        merge_far, out_shape=packed(Y * CORES, NEAR * HEADS, LANES), in_specs=[vmem], out_specs=vmem,
+        merge_far, out_shape=packed(TOKENS, HEADS, LANES), in_specs=[vmem], out_specs=vmem,
         compiler_params=small_params, name="merge_far"
     )(parts)
-    rows = lax.all_to_all(copies, ("y", "core"), 0, 0, axis_index_groups=[gather_order], tiled=True)
+    rows = lax.all_to_all(copies, near_axes, 0, 0, axis_index_groups=near_order, tiled=True)
     copies = pl.pallas_call(
         project,
         out_shape=packed(HEAD, TOKENS * COLS // LANES, LANES),

time: 50.9 us -> 49.7 us (0.976)
  blocking collectives: 46.8 us -> 46 us
    all_to_all x3, blocking collectives: 40.2 us -> 39.1 us  [the longest x1 15.1 us: shards(): lax.all_to_all(copies, 'far', 0, 0, axis_index_groups=far_order, tiled=True)]
where the time goes in v7:
time: 49.7 us; the launch traced here: 49.5 us
  blocking collectives  46 us (93%)
  Pallas kernels  3.47 us (7%)
    all_to_all x1, blocking collectives, shards(): lax.all_to_all(copies, 'far', 0, 0, axis_index_groups=far_order, tiled=True)  15.1 us
    all_to_all x1, blocking collectives, shards(): lax.all_to_all(block, near_axes, 0, 0, axis_index_groups=near_order, tile...  14.4 us
    all_to_all x1, blocking collectives, shards(): lax.all_to_all(copies, near_axes, 0, 0, axis_index_groups=near_order, til...  9.69 us
    all_to_all x1, blocking collectives, shards(): lax.all_to_all(copies, 'head', 0, 0, axis_index_groups=head_order, tiled=...  6.87 us
    pallas_call x1, Pallas kernels, shards(): pl.pallas_call(attend_block, out_shape=packed(TOKENS, 1, MESSAGE), in_spe...  2.24 us

profile of v7, /device:TPU:1, one launch (start us, length us, event | category | flops | bytes accessed | tf_op | source)
XLA Modules:
  0.0 49.5 jit_solution(5982888387498258499)
XLA Ops:
  0.0 2.2 %attend_block.1 = f32[16,1,1152]{2,1,0:T(1,128)S(1)} custom-call(s32[4]{0:T(128)} %lengths.1, s32[4,4]{1,0:T(4,128)} %offsets.1, bf16[4,1,32,128]{3,2,1,0:T(8,128)(2,1)} %bitcast.5, bf16[4,1,128,1024]{3,2,1,0:T(8,128)(2,1)} %keys.1, bf16[4,1,128,1024]{3,2,1,0:T(8,128)(2,1)} %values.1), custom_call_target="tpu_custom_call" | custom-call | tf_op jit(solution)/shard_map/attend_block/pallas_call | solution.py:134
  2.2 14.4 %all_to_all.20.parts = f32[16,1,1152]{2,1,0:T(1,128)S(1)} all-to-all(f32[16,1,1152]{2,1,0:T(1,128)S(1)} %attend_block.1), channel_id=1, replica_groups={{268,0,4,8,12,128,132,136,140,256,260,264,384,388,392,396},{269,1,5,9,1..., dimensions={0} | all-to-all | bytes 147456 | tf_op jit(solution)/shard_map/all_to_all | solution.py:152
  16.6 0.2 merge_near.1
  16.8 15.1 %all_to_all.21.parts = f32[8,1,1152]{2,1,0:T(1,128)S(1)} all-to-all(f32[8,1,1152]{2,1,0:T(1,128)S(1)} %merge_near.1), channel_id=1, replica_groups={{80,96,112,0,16,32,48,64},{81,97,113,1,17,33,49,65},{82,98,114,2,18,34,..., dimensions={0} | all-to-all | bytes 73728 | tf_op jit(solution)/shard_map/all_to_all | solution.py:157
  31.8 0.0 copy-start
  31.8 0.2 merge_far.1
  32.0 9.7 %all_to_all.22 = f32[16,8,128]{2,1,0:T(8,128)S(1)} all-to-all(f32[16,8,128]{2,1,0:T(8,128)S(1)} %merge_far.1), channel_id=1, replica_groups={{268,0,4,8,12,128,132,136,140,256,260,264,384,388,392,396},{269,1,5,9,1..., dimensions={0} | all-to-all | bytes 131072 | tf_op jit(solution)/shard_map/all_to_all | solution.py:162
  41.7 0.0 copy-done
  41.7 0.2 project.1
  42.0 6.9 %all_to_all.23.terms = f32[4,8,128]{2,1,0:T(8,128)S(1)} all-to-all(f32[4,8,128]{2,1,0:T(8,128)S(1)} %project.1), channel_id=1, replica_groups={{2,3,0,1},{6,7,4,5},{10,11,8,9},{14,15,12,13},{18,19,16,17},{22,23,20,2..., dimensions={0} | all-to-all | bytes 32768 | tf_op jit(solution)/shard_map/all_to_all | solution.py:171
  48.8 0.7 %add_groups.1 = f32[4,4,64]{2,1,0:T(4,128)} custom-call(f32[4,8,128]{2,1,0:T(8,128)S(1)} %all_to_all.23.terms), custom_call_target="tpu_custom_call" | custom-call | tf_op jit(solution)/shard_map/add_groups/pallas_call | solution.py:172
Async XLA Ops:
  31.8 9.9 %copy-start = (bf16[1,8,128,64]{2,3,1,0:T(8,128)(2,1)S(1)}, bf16[1,8,128,64]{2,3,1,0:T(8,128)(2,1)}, u32[]{:S(2)}) copy-start(bf16[1,8,128,64]{2,3,1,0:T(8,128)(2,1)} %param.11) | copy-start | bytes 393220

commit v8 on v7

--- a/solution.py
+++ b/solution.py
@@ -13,7 +13,7 @@
 SLOT = LANES // HEADS
 MESSAGE = (HEADS + 1) * LANES
 near_order = [[11, 0, 1, 2, 3, 4, 5, 6, 7, 8, 9, 10, 12, 13, 14, 15]]
-far_order = [[5, 6, 7, 0, 1, 2, 3, 4]]
+far_order = [[10, 12, 14, 0, 2, 4, 6, 8], [9, 11, 13, 15, 1, 3, 5, 7]]
 head_order = [[2, 3, 0, 1]]
 near_axes = ("y", "near", "core")
 vmem = pl.BlockSpec(memory_space=pltpu.VMEM)
@@ -154,7 +154,9 @@
         merge_near, out_shape=packed(FAR, 1, MESSAGE), in_specs=[vmem], out_specs=vmem,
         compiler_params=small_params, name="merge_near"
     )(parts)
-    parts = lax.all_to_all(copies, "far", 0, 0, axis_index_groups=far_order, tiled=True)
+    parts = lax.all_to_all(
+        copies, ("far", "near"), 0, 0, axis_index_groups=far_order, tiled=True
+    )
     copies = pl.pallas_call(
         merge_far, out_shape=packed(TOKENS, HEADS, LANES), in_specs=[vmem], out_specs=vmem,
         compiler_params=small_params, name="merge_far"

time: 49.7 us -> 49.8 us (level)
  no operation moved by 1% of the time
where the time goes in v8:
time: 49.8 us; the launch traced here: 49.5 us
  blocking collectives  46 us (92%)
  Pallas kernels  3.47 us (7%)
    all_to_all x1, blocking collectives, shards(): lax.all_to_all(copies, ('far', 'near'), 0, 0, axis_index_groups=far_order...  15.1 us
    all_to_all x1, blocking collectives, shards(): lax.all_to_all(block, near_axes, 0, 0, axis_index_groups=near_order, tile...  14.4 us
    all_to_all x1, blocking collectives, shards(): lax.all_to_all(copies, near_axes, 0, 0, axis_index_groups=near_order, til...  9.72 us
    all_to_all x1, blocking collectives, shards(): lax.all_to_all(copies, 'head', 0, 0, axis_index_groups=head_order, tiled=...  6.87 us
    pallas_call x1, Pallas kernels, shards(): pl.pallas_call(attend_block, out_shape=packed(TOKENS, 1, MESSAGE), in_spe...  2.24 us

profile of v8, /device:TPU:1, one launch (start us, length us, event | category | flops | bytes accessed | tf_op | source)
XLA Modules:
  0.0 49.5 jit_solution(17500453866432070003)
XLA Ops:
  0.0 2.2 %attend_block.1 = f32[16,1,1152]{2,1,0:T(1,128)S(1)} custom-call(s32[4]{0:T(128)} %lengths.1, s32[4,4]{1,0:T(4,128)} %offsets.1, bf16[4,1,32,128]{3,2,1,0:T(8,128)(2,1)} %bitcast.5, bf16[4,1,128,1024]{3,2,1,0:T(8,128)(2,1)} %keys.1, bf16[4,1,128,1024]{3,2,1,0:T(8,128)(2,1)} %values.1), custom_call_target="tpu_custom_call" | custom-call | tf_op jit(solution)/shard_map/attend_block/pallas_call | solution.py:134
  2.2 14.4 %all_to_all.20.parts = f32[16,1,1152]{2,1,0:T(1,128)S(1)} all-to-all(f32[16,1,1152]{2,1,0:T(1,128)S(1)} %attend_block.1), channel_id=1, replica_groups={{268,0,4,8,12,128,132,136,140,256,260,264,384,388,392,396},{269,1,5,9,1..., dimensions={0} | all-to-all | bytes 147456 | tf_op jit(solution)/shard_map/all_to_all | solution.py:152
  16.6 0.2 merge_near.1
  16.8 15.1 %all_to_all.21.parts = f32[8,1,1152]{2,1,0:T(1,128)S(1)} all-to-all(f32[8,1,1152]{2,1,0:T(1,128)S(1)} %merge_near.1), channel_id=1, replica_groups={{80,96,112,0,16,32,48,64},{72,88,104,120,8,24,40,56},{81,97,113,1,17,33..., dimensions={0} | all-to-all | bytes 73728 | tf_op jit(solution)/shard_map/all_to_all | solution.py:157
  31.8 0.0 copy-start
  31.8 0.2 merge_far.1
  32.0 9.7 %all_to_all.22 = f32[16,8,128]{2,1,0:T(8,128)S(1)} all-to-all(f32[16,8,128]{2,1,0:T(8,128)S(1)} %merge_far.1), channel_id=1, replica_groups={{268,0,4,8,12,128,132,136,140,256,260,264,384,388,392,396},{269,1,5,9,1..., dimensions={0} | all-to-all | bytes 131072 | tf_op jit(solution)/shard_map/all_to_all | solution.py:164
  41.7 0.0 copy-done
  41.7 0.2 project.1
  42.0 6.9 %all_to_all.23.terms = f32[4,8,128]{2,1,0:T(8,128)S(1)} all-to-all(f32[4,8,128]{2,1,0:T(8,128)S(1)} %project.1), channel_id=1, replica_groups={{2,3,0,1},{6,7,4,5},{10,11,8,9},{14,15,12,13},{18,19,16,17},{22,23,20,2..., dimensions={0} | all-to-all | bytes 32768 | tf_op jit(solution)/shard_map/all_to_all | solution.py:173
  48.9 0.7 %add_groups.1 = f32[4,4,64]{2,1,0:T(4,128)} custom-call(f32[4,8,128]{2,1,0:T(8,128)S(1)} %all_to_all.23.terms), custom_call_target="tpu_custom_call" | custom-call | tf_op jit(solution)/shard_map/add_groups/pallas_call | solution.py:174
Async XLA Ops:
  31.8 9.9 %copy-start = (bf16[1,8,128,64]{2,3,1,0:T(8,128)(2,1)S(1)}, bf16[1,8,128,64]{2,3,1,0:T(8,128)(2,1)}, u32[]{:S(2)}) copy-start(bf16[1,8,128,64]{2,3,1,0:T(8,128)(2,1)} %param.11) | copy-start | bytes 393220

commit v9 on v8

--- a/solution.py
+++ b/solution.py
@@ -54,7 +54,7 @@
     ]
     key_copy = pltpu.make_async_copy(keys, held_keys, key_sem)
     value_copy = pltpu.make_async_copy(values, held_values, value_sem)
-    for copy in small + [key_copy, value_copy]:
+    for copy in [key_copy, *small, value_copy]:
         copy.start()
     chip = (lax.axis_index("y") * FAR + lax.axis_index("far")) * NEAR + lax.axis_index("near")
     index = chip * CORES + lax.axis_index("core")

time: 49.8 us -> 49.8 us (level)
  no operation moved by 1% of the time
where the time goes in v9:
time: 49.8 us; the launch traced here: 49.5 us
  blocking collectives  46 us (92%)
  Pallas kernels  3.47 us (7%)
    all_to_all x1, blocking collectives, shards(): lax.all_to_all(copies, ('far', 'near'), 0, 0, axis_index_groups=far_order...  15.1 us
    all_to_all x1, blocking collectives, shards(): lax.all_to_all(block, near_axes, 0, 0, axis_index_groups=near_order, tile...  14.4 us
    all_to_all x1, blocking collectives, shards(): lax.all_to_all(copies, near_axes, 0, 0, axis_index_groups=near_order, til...  9.72 us
    all_to_all x1, blocking collectives, shards(): lax.all_to_all(copies, 'head', 0, 0, axis_index_groups=head_order, tiled=...  6.87 us
    pallas_call x1, Pallas kernels, shards(): pl.pallas_call(attend_block, out_shape=packed(TOKENS, 1, MESSAGE), in_spe...  2.24 us

profile of v9, /device:TPU:1, one launch (start us, length us, event | category | flops | bytes accessed | tf_op | source)
XLA Modules:
  0.0 49.5 jit_solution(5639390103116895650)
XLA Ops:
  0.0 2.2 %attend_block.1 = f32[16,1,1152]{2,1,0:T(1,128)S(1)} custom-call(s32[4]{0:T(128)} %lengths.1, s32[4,4]{1,0:T(4,128)} %offsets.1, bf16[4,1,32,128]{3,2,1,0:T(8,128)(2,1)} %bitcast.5, bf16[4,1,128,1024]{3,2,1,0:T(8,128)(2,1)} %keys.1, bf16[4,1,128,1024]{3,2,1,0:T(8,128)(2,1)} %values.1), custom_call_target="tpu_custom_call" | custom-call | tf_op jit(solution)/shard_map/attend_block/pallas_call | solution.py:134
  2.2 14.4 %all_to_all.20.parts = f32[16,1,1152]{2,1,0:T(1,128)S(1)} all-to-all(f32[16,1,1152]{2,1,0:T(1,128)S(1)} %attend_block.1), channel_id=1, replica_groups={{268,0,4,8,12,128,132,136,140,256,260,264,384,388,392,396},{269,1,5,9,1..., dimensions={0} | all-to-all | bytes 147456 | tf_op jit(solution)/shard_map/all_to_all | solution.py:152
  16.6 0.2 merge_near.1
  16.8 15.1 %all_to_all.21.parts = f32[8,1,1152]{2,1,0:T(1,128)S(1)} all-to-all(f32[8,1,1152]{2,1,0:T(1,128)S(1)} %merge_near.1), channel_id=1, replica_groups={{80,96,112,0,16,32,48,64},{72,88,104,120,8,24,40,56},{81,97,113,1,17,33..., dimensions={0} | all-to-all | bytes 73728 | tf_op jit(solution)/shard_map/all_to_all | solution.py:157
  31.8 0.0 copy-start
  31.8 0.2 merge_far.1
  32.0 9.7 %all_to_all.22 = f32[16,8,128]{2,1,0:T(8,128)S(1)} all-to-all(f32[16,8,128]{2,1,0:T(8,128)S(1)} %merge_far.1), channel_id=1, replica_groups={{268,0,4,8,12,128,132,136,140,256,260,264,384,388,392,396},{269,1,5,9,1..., dimensions={0} | all-to-all | bytes 131072 | tf_op jit(solution)/shard_map/all_to_all | solution.py:164
  41.7 0.0 copy-done
  41.7 0.2 project.1
  42.0 6.9 %all_to_all.23.terms = f32[4,8,128]{2,1,0:T(8,128)S(1)} all-to-all(f32[4,8,128]{2,1,0:T(8,128)S(1)} %project.1), channel_id=1, replica_groups={{2,3,0,1},{6,7,4,5},{10,11,8,9},{14,15,12,13},{18,19,16,17},{22,23,20,2..., dimensions={0} | all-to-all | bytes 32768 | tf_op jit(solution)/shard_map/all_to_all | solution.py:173
  48.9 0.7 %add_groups.1 = f32[4,4,64]{2,1,0:T(4,128)} custom-call(f32[4,8,128]{2,1,0:T(8,128)S(1)} %all_to_all.23.terms), custom_call_target="tpu_custom_call" | custom-call | tf_op jit(solution)/shard_map/add_groups/pallas_call | solution.py:174
Async XLA Ops:
  31.8 9.9 %copy-start = (bf16[1,8,128,64]{2,3,1,0:T(8,128)(2,1)S(1)}, bf16[1,8,128,64]{2,3,1,0:T(8,128)(2,1)}, u32[]{:S(2)}) copy-start(bf16[1,8,128,64]{2,3,1,0:T(8,128)(2,1)} %param.11) | copy-start | bytes 393220
